TPU v7x, 512 devices: a whole 4x8x8 slice. The times are simulated.
512 devices in a mesh: tm: 8 (over z), gx: 8 (over y_hi, x), gy: 8 (over y_lo, core).
Axes of the slice: x: 4, y: 8 (y_hi: 2, y_lo: 4; y = y_hi * 4 + y_lo), z: 8, core: 2. Of those that a mesh axis runs over, the one named last changes fastest.
Arguments:
- states: float32 [16, 512, 1024], P('tm', 'gx', 'gy'), may hold values from 0.5 to 1.5
- bed: float32 [512, 1024], P('gx', 'gy'), may hold values from -3 to 3
- background_state: float32 [512, 1024], P('gx', 'gy'), may hold values from 0.5 to 1.5
- ice_mask: int32 [512, 1024], P('gx', 'gy'), may hold values 0 or 1
- flow_rate: float32 [512, 1024], P('gx', 'gy'), may hold values from 0.02 to 0.1
- obs_cell: int32 [16, 8, 8, 512], P('tm', 'gx', 'gy'), may hold values from 0 to 8191
- obs_value: float32 [16, 8, 8, 512], P('tm', 'gx', 'gy'), may hold values from 0.5 to 1.5
Outputs:
- states_out: float32 [16, 512, 1024], P('tm', 'gx', 'gy')
- bed_out: float32 [512, 1024], P('gx', 'gy')
All inputs are finite; a program needn't handle non-finite values. No bound on the sum of `ice_mask` on one device may be relied on, other than what follows from the above.
Results may differ from a plain program's by a relative error of at most 0.0001.
Values sent between devices are 32-bit elements; how exact they have to be, the bound alone decides.
A program may use at most 64 MiB of HBM per device.

v0:
```python
import jax
import jax.numpy as jnp
from jax import lax
from jax.sharding import PartitionSpec as P

STEPS = 4
OUTER = 2


bed_rate = 0.1
state_rate = 0.5


def with_halo(value, sides, width):
    for axis, dim in sides:
        count, length = (lax.axis_size(axis), value.shape[dim])
        up = [(i, (i + 1) % count) for i in range(count - 1)]
        down = [(j, i) for i, j in up]
        last = lax.slice_in_dim(value, length - width, length, axis=dim)
        first = lax.slice_in_dim(value, 0, width, axis=dim)
        before = lax.ppermute(last, axis, up)
        after = lax.ppermute(first, axis, down)
        value = jnp.concatenate([before, value, after], axis=dim)
    return value


def from_behind(block, axis, distance):
    devices = range(lax.axis_size(axis))
    route = [(i - distance, i) for i in devices if i - distance in devices]
    return lax.ppermute(block, axis, route)


def sent_to_all(value, axis):
    copies = jnp.broadcast_to(value, (lax.axis_size(axis), *value.shape))
    return lax.all_to_all(copies, axis, split_axis=0, concat_axis=0, tiled=True)


def taken_together(value, axis):
    return sent_to_all(value, axis).sum(axis=0)


def advance(thick, ground, maskf, rate):
    surface = ground + thick
    open_x = maskf[1:, :] * maskf[:-1, :]
    coef_x = 0.5 * (rate[1:, :] + rate[:-1, :]) * open_x
    mean_x = 0.5 * (thick[1:, :] + thick[:-1, :])
    flux_x = coef_x * mean_x * mean_x * (surface[1:, :] - surface[:-1, :])
    open_y = maskf[:, 1:] * maskf[:, :-1]
    coef_y = 0.5 * (rate[:, 1:] + rate[:, :-1]) * open_y
    mean_y = 0.5 * (thick[:, 1:] + thick[:, :-1])
    flux_y = coef_y * mean_y * mean_y * (surface[:, 1:] - surface[:, :-1])
    change = flux_x[1:, 1:-1] - flux_x[:-1, 1:-1] + (flux_y[1:-1, 1:] - flux_y[1:-1, :-1])
    return thick[1:-1, 1:-1] + change


def batch_advance(thick, ground, maskf, rate):
    return jax.vmap(advance, in_axes=(0, None, None, None))(thick, ground, maskf, rate)


def inner(array, width):
    return array[..., width : array.shape[-2] - width, width : array.shape[-1] - width]


def per_device(states, bed, background_state, ice_mask, flow_rate, obs_cell, obs_value):
    slices_here, rows_here, cols_here = states.shape
    maskf = ice_mask.astype(jnp.float32)
    offsets = (jnp.arange(slices_here, dtype=jnp.int32) * (rows_here * cols_here))[:, None]
    cell_index = (obs_cell.reshape(slices_here, -1) + offsets).reshape(-1)
    observed = obs_value.reshape(-1)
    first_device = lax.axis_index("tm") == 0
    reach = 2 * STEPS
    mask_pad, rate_pad = (
        with_halo(maskf, (("gx", 0), ("gy", 1)), reach),
        with_halo(flow_rate, (("gx", 0), ("gy", 1)), reach),
    )
    bed_prior = bed
    for outer in range(OUTER):
        wide_path = []
        stacked = jnp.concatenate([bed[None], states], axis=0)
        wide = with_halo(stacked, (("gx", 1), ("gy", 2)), reach)
        bed_pad = wide[0]
        walker = wide[1:]
        for step in range(STEPS):
            wide_path.append(walker)
            walker = batch_advance(
                walker, inner(bed_pad, step), inner(mask_pad, step), inner(rate_pad, step)
            )
        final = inner(walker, STEPS)
        incoming = from_behind(final[slices_here - 1], "tm", 1)
        start_state = jnp.where(first_device, background_state, incoming)
        previous = jnp.concatenate([start_state[None], final[:-1]], axis=0)
        misfit = states - previous
        later = from_behind(misfit[0], "tm", -1)
        following = jnp.concatenate([misfit[1:], later[None]], axis=0)
        predicted = final.reshape(-1)[cell_index]
        residual = predicted - observed
        spread = (
            jnp.zeros((slices_here * rows_here * cols_here,), jnp.float32)
            .at[cell_index]
            .add(residual)
        )
        adjoint = spread.reshape(slices_here, rows_here, cols_here) - following
        bed_grad = jnp.zeros((rows_here, cols_here), jnp.float32)
        wide_adjoint = with_halo(adjoint, (("gx", 1), ("gy", 2)), STEPS)
        for step in reversed(range(STEPS)):
            radius = step + 1
            thick_in = inner(wide_path[step], reach - step - (radius + 1))
            cut = reach - (radius + 1)
            mask_here = inner(mask_pad, cut)
            rate_here = inner(rate_pad, cut)

            def wide_step(thick_arg, ground_arg):
                return batch_advance(thick_arg, ground_arg, mask_here, rate_here)

            _, pull = jax.vjp(wide_step, thick_in, inner(bed_pad, cut))
            grad_thick, grad_ground = pull(wide_adjoint)
            wide_adjoint = inner(grad_thick, 2)
            bed_grad = bed_grad + inner(grad_ground, radius + 1)
        adjoint = wide_adjoint
        total = taken_together(bed_grad, "tm")
        bed = bed - bed_rate * (total + (bed - bed_prior))
        states = states - state_rate * (misfit + adjoint)
    return (states, bed)


def solution(mesh):
    placed = (
        P("tm", "gx", "gy"),
        P("gx", "gy"),
        P("gx", "gy"),
        P("gx", "gy"),
        P("gx", "gy"),
        P("tm", "gx", "gy", None),
        P("tm", "gx", "gy", None),
    )
    return jax.shard_map(
        per_device,
        mesh=mesh,
        in_specs=placed,
        out_specs=(P("tm", "gx", "gy"), P("gx", "gy")),
        check_vma=False,
    )
```

profile of v0, /device:TPU:56, one launch (start us, length us, event | category | flops | bytes accessed | tf_op | source)
XLA Modules:
  0.0 216.8 jit_solution(735727196775739109)
XLA Ops:
  1.4 7.0 %collective-permute-start.9 = (f32[8,128]{1,0:T(8,128)S(1)}, f32[8,128]{1,0:T(8,128)S(1)}, u32[]{:S(2)}, u32[]{:S(2)}) collective-permute-start(f32[8,128]{1,0:T(8,128)S(1)} %get-tuple-element.141), channel_id=1, source_target_pairs={{8,0},{16,8},{24,16},{32,24},{40,32},{48,40},{56,48},{9,1},{17,9},... | collective-permute-start | bytes 12296 | tf_op jit(solution)/shard_map/ppermute | solution.py:22
  13.0 9.9 %collective-permute-start.5 = (f32[8,128]{1,0:T(8,128)S(1)}, f32[8,128]{1,0:T(8,128)S(1)}, u32[]{:S(2)}, u32[]{:S(2)}) collective-permute-start(f32[8,128]{1,0:T(8,128)S(1)} %get-tuple-element.138), channel_id=1, source_target_pairs={{8,0},{16,8},{24,16},{32,24},{40,32},{48,40},{56,48},{9,1},{17,9},... | collective-permute-start | bytes 12296 | tf_op jit(solution)/shard_map/ppermute | solution.py:22
  23.0 3.9 %collective-permute-start.1 = (f32[3,8,128]{2,1,0:T(8,128)S(1)}, f32[3,8,128]{2,1,0:T(8,128)S(1)}, u32[]{:S(2)}, u32[]{:S(2)}) collective-permute-start(f32[3,8,128]{2,1,0:T(8,128)S(1)} %get-tuple-element.121), channel_id=1, source_target_pairs={{8,0},{16,8},{24,16},{32,24},{40,32},{48,40},{56,48},{9,1},{17,9},... | collective-permute-start | bytes 36872 | tf_op jit(solution)/shard_map/ppermute | solution.py:22
  34.3 3.2 %collective-permute-start.7 = (f32[80,8]{1,0:T(8,128)S(1)}, f32[80,8]{1,0:T(8,128)S(1)}, u32[]{:S(2)}, u32[]{:S(2)}) collective-permute-start(f32[80,8]{1,0:T(8,128)S(1)} %get-tuple-element.135), channel_id=1, source_target_pairs={{1,0},{2,1},{3,2},{4,3},{5,4},{6,5},{7,6},{9,8},{10,9},{11,10},{12... | collective-permute-start | bytes 7688 | tf_op jit(solution)/shard_map/ppermute | solution.py:22
  39.5 3.3 %collective-permute-done.6 = f32[80,8]{1,0:T(8,128)S(1)} collective-permute-done((f32[80,8]{1,0:T(8,128)S(1)}, f32[80,8]{1,0:T(8,128)S(1)}, u32[]{:S(2)}, u32[]{:S(2)}) %collective-permute-start.6) | collective-permute-done | bytes 2592 | tf_op jit(solution)/shard_map/ppermute | solution.py:21
  49.2 3.6 %collective-permute-done.2 = f32[3,80,8]{2,1,0:T(8,128)S(1)} collective-permute-done((f32[3,80,8]{2,1,0:T(8,128)S(1)}, f32[3,80,8]{2,1,0:T(8,128)S(1)}, u32[]{:S(2)}, u32[]{:S(2)}) %collective-permute-start.2) | collective-permute-done | bytes 7712 | tf_op jit(solution)/shard_map/ppermute | solution.py:21
  55.3 4.3 %collective-permute-start.12 = (f32[64,128]{1,0:T(8,128)S(1)}, f32[64,128]{1,0:T(8,128)S(1)}, u32[]{:S(2)}, u32[]{:S(2)}) collective-permute-start(f32[64,128]{1,0:T(8,128)S(1)} %get-tuple-element.112), channel_id=1, source_target_pairs={{0,64},{64,128},{128,192},{192,256},{256,320},{320,384},{384,448},... | collective-permute-start | bytes 98312 | tf_op jit(solution)/shard_map/ppermute | solution.py:30
  62.8 6.2 %gather_fusion = f32[1024]{0:T(1024)S(1)} fusion(f32[16384]{0:T(1024)S(1)} %bitcast.34, s32[1024]{0:T(1024)S(1)} %broadcast_clamp_fusion), kind=kCustom, calls=%fused_computation | custom fusion | bytes 12288 | tf_op jit(solution)/shard_map/gather | solution.py:95
  69.0 5.9 %scatter_custom_fusion = f32[16384]{0:T(1024)S(1)} fusion(s32[1024]{0:T(1024)S(1)} %bitcast.45, f32[1024]{0:T(1024)S(1)} %sub.189, f32[]{:T(128)} %constant.12.clone.1), kind=kCustom, calls=%fused_computation.342 | custom fusion | flops 1024 | bytes 65540 | tf_op jit(solution)/shard_map/scatter-add | solution.py:100
  75.0 9.9 %collective-permute-start.15 = (f32[2,4,128]{2,1,0:T(4,128)S(1)}, f32[2,4,128]{2,1,0:T(4,128)S(1)}, u32[]{:S(2)}, u32[]{:S(2)}) collective-permute-start(f32[2,4,128]{2,1,0:T(4,128)S(1)} %get-tuple-element.131), channel_id=1, source_target_pairs={{8,0},{16,8},{24,16},{32,24},{40,32},{48,40},{56,48},{9,1},{17,9},... | collective-permute-start | bytes 12296 | tf_op jit(solution)/shard_map/ppermute | solution.py:22
  87.1 9.4 %collective-permute-done.14 = f32[2,4,128]{2,1,0:T(4,128)S(1)} collective-permute-done((f32[2,4,128]{2,1,0:T(4,128)S(1)}, f32[2,4,128]{2,1,0:T(4,128)S(1)}, u32[]{:S(2)}, u32[]{:S(2)}) %collective-permute-start.14) | collective-permute-done | bytes 4128 | tf_op jit(solution)/shard_map/ppermute | solution.py:21
  101.0 3.1 %collective-permute-done.16 = f32[2,72,4]{2,1,0:T(8,128)S(1)} collective-permute-done((f32[2,72,4]{2,1,0:T(8,128)S(1)}, f32[2,72,4]{2,1,0:T(8,128)S(1)}, u32[]{:S(2)}, u32[]{:S(2)}) %collective-permute-start.16) | collective-permute-done | bytes 2336 | tf_op jit(solution)/shard_map/ppermute | solution.py:21
  108.3 12.6 %all-to-all-start = ((f32[8,64,128]{2,1,0:T(8,128)}), f32[8,64,128]{2,1,0:T(8,128)S(1)}, u32[]{:S(2)}, u32[]{:S(2)}) async-start(f32[8,64,128]{2,1,0:T(8,128)} %broadcast_in_dim.19), calls=%async_computation | async-start | bytes 524288 | tf_op jit(solution)/shard_map/all_to_all | solution.py:35
  121.1 10.3 %all-to-all-done = f32[8,64,128]{2,1,0:T(8,128)S(1)} async-done(((f32[8,64,128]{2,1,0:T(8,128)}), f32[8,64,128]{2,1,0:T(8,128)S(1)}, u32[]{:S(2)}, u32[]{:S(2)}) %all-to-all-start) | async-done | bytes 262176 | tf_op jit(solution)/shard_map/all_to_all | solution.py:35
  133.4 3.9 %collective-permute-start.18 = (f32[3,8,128]{2,1,0:T(8,128)S(1)}, f32[3,8,128]{2,1,0:T(8,128)S(1)}, u32[]{:S(2)}, u32[]{:S(2)}) collective-permute-start(f32[3,8,128]{2,1,0:T(8,128)S(1)} %get-tuple-element.118), channel_id=1, source_target_pairs={{0,8},{8,16},{16,24},{24,32},{32,40},{40,48},{48,56},{1,9},{9,17},... | collective-permute-start | bytes 36872 | tf_op jit(solution)/shard_map/ppermute | solution.py:21
  137.3 7.7 %collective-permute-done.18 = f32[3,8,128]{2,1,0:T(8,128)S(1)} collective-permute-done((f32[3,8,128]{2,1,0:T(8,128)S(1)}, f32[3,8,128]{2,1,0:T(8,128)S(1)}, u32[]{:S(2)}, u32[]{:S(2)}) %collective-permute-start.18) | collective-permute-done | bytes 12320 | tf_op jit(solution)/shard_map/ppermute | solution.py:21
  149.6 3.6 %collective-permute-done.20 = f32[3,80,8]{2,1,0:T(8,128)S(1)} collective-permute-done((f32[3,80,8]{2,1,0:T(8,128)S(1)}, f32[3,80,8]{2,1,0:T(8,128)S(1)}, u32[]{:S(2)}, u32[]{:S(2)}) %collective-permute-start.20) | collective-permute-done | bytes 7712 | tf_op jit(solution)/shard_map/ppermute | solution.py:21
  161.4 6.2 %gather_fusion.1 = f32[1024]{0:T(1024)S(1)} fusion(f32[16384]{0:T(1024)S(1)} %bitcast.33, s32[1024]{0:T(1024)S(1)} %broadcast_clamp_fusion), kind=kCustom, calls=%fused_computation.1 | custom fusion | bytes 12288 | tf_op jit(solution)/shard_map/gather | solution.py:95
  167.6 5.9 %scatter_custom_fusion.1 = f32[16384]{0:T(1024)S(1)} fusion(s32[1024]{0:T(1024)S(1)} %bitcast.46, f32[1024]{0:T(1024)S(1)} %sub.217, f32[]{:T(128)} %constant.12.clone.1), kind=kCustom, calls=%fused_computation.340 | custom fusion | flops 1024 | bytes 65540 | tf_op jit(solution)/shard_map/scatter-add | solution.py:100
  175.5 3.9 %collective-permute-start.24 = (f32[2,4,128]{2,1,0:T(4,128)S(1)}, f32[2,4,128]{2,1,0:T(4,128)S(1)}, u32[]{:S(2)}, u32[]{:S(2)}) collective-permute-start(f32[2,4,128]{2,1,0:T(4,128)S(1)} %get-tuple-element.126), channel_id=1, source_target_pairs={{0,8},{8,16},{16,24},{24,32},{32,40},{40,48},{48,56},{1,9},{9,17},... | collective-permute-start | bytes 12296 | tf_op jit(solution)/shard_map/ppermute | solution.py:21
  179.6 7.4 %collective-permute-done.24 = f32[2,4,128]{2,1,0:T(4,128)S(1)} collective-permute-done((f32[2,4,128]{2,1,0:T(4,128)S(1)}, f32[2,4,128]{2,1,0:T(4,128)S(1)}, u32[]{:S(2)}, u32[]{:S(2)}) %collective-permute-start.24) | collective-permute-done | bytes 4128 | tf_op jit(solution)/shard_map/ppermute | solution.py:21
  191.6 3.1 %collective-permute-done.26 = f32[2,72,4]{2,1,0:T(8,128)S(1)} collective-permute-done((f32[2,72,4]{2,1,0:T(8,128)S(1)}, f32[2,72,4]{2,1,0:T(8,128)S(1)}, u32[]{:S(2)}, u32[]{:S(2)}) %collective-permute-start.26) | collective-permute-done | bytes 2336 | tf_op jit(solution)/shard_map/ppermute | solution.py:21
  198.8 6.8 %all-to-all-start.1 = ((f32[8,64,128]{2,1,0:T(8,128)}), f32[8,64,128]{2,1,0:T(8,128)S(1)}, u32[]{:S(2)}, u32[]{:S(2)}) async-start(f32[8,64,128]{2,1,0:T(8,128)} %broadcast_in_dim.23), calls=%async_computation.1 | async-start | bytes 524288 | tf_op jit(solution)/shard_map/all_to_all | solution.py:35
  206.5 9.7 %all-to-all-done.1 = f32[8,64,128]{2,1,0:T(8,128)S(1)} async-done(((f32[8,64,128]{2,1,0:T(8,128)}), f32[8,64,128]{2,1,0:T(8,128)S(1)}, u32[]{:S(2)}, u32[]{:S(2)}) %all-to-all-start.1) | async-done | bytes 262176 | tf_op jit(solution)/shard_map/all_to_all | solution.py:35
  (198 shorter events, 64.0 us)
Async XLA Ops:
  1.4 26.3 %collective-permute-start.9 = (f32[8,128]{1,0:T(8,128)S(1)}, f32[8,128]{1,0:T(8,128)S(1)}, u32[]{:S(2)}, u32[]{:S(2)}) collective-permute-start(f32[8,128]{1,0:T(8,128)S(1)} %get-tuple-element.141), channel_id=1, source_target_pairs={{8,0},{16,8},{24,16},{32,24},{40,32},{48,40},{56,48},{9,1},{17,9},... | collective-permute-start | bytes 12296 | tf_op jit(solution)/shard_map/ppermute | solution.py:22
  8.5 21.2 %collective-permute-start.8 = (f32[8,128]{1,0:T(8,128)S(1)}, f32[8,128]{1,0:T(8,128)S(1)}, u32[]{:S(2)}, u32[]{:S(2)}) collective-permute-start(f32[8,128]{1,0:T(8,128)S(1)} %get-tuple-element.140), channel_id=1, source_target_pairs={{0,8},{8,16},{16,24},{24,32},{32,40},{40,48},{48,56},{1,9},{9,17},... | collective-permute-start | bytes 12296 | tf_op jit(solution)/shard_map/ppermute | solution.py:21
  11.1 20.6 %collective-permute-start.4 = (f32[8,128]{1,0:T(8,128)S(1)}, f32[8,128]{1,0:T(8,128)S(1)}, u32[]{:S(2)}, u32[]{:S(2)}) collective-permute-start(f32[8,128]{1,0:T(8,128)S(1)} %get-tuple-element.139), channel_id=1, source_target_pairs={{0,8},{8,16},{16,24},{24,32},{32,40},{40,48},{48,56},{1,9},{9,17},... | collective-permute-start | bytes 12296 | tf_op jit(solution)/shard_map/ppermute | solution.py:21
  13.0 21.1 %collective-permute-start.5 = (f32[8,128]{1,0:T(8,128)S(1)}, f32[8,128]{1,0:T(8,128)S(1)}, u32[]{:S(2)}, u32[]{:S(2)}) collective-permute-start(f32[8,128]{1,0:T(8,128)S(1)} %get-tuple-element.138), channel_id=1, source_target_pairs={{8,0},{16,8},{24,16},{32,24},{40,32},{48,40},{56,48},{9,1},{17,9},... | collective-permute-start | bytes 12296 | tf_op jit(solution)/shard_map/ppermute | solution.py:22
  23.0 21.6 %collective-permute-start.1 = (f32[3,8,128]{2,1,0:T(8,128)S(1)}, f32[3,8,128]{2,1,0:T(8,128)S(1)}, u32[]{:S(2)}, u32[]{:S(2)}) collective-permute-start(f32[3,8,128]{2,1,0:T(8,128)S(1)} %get-tuple-element.121), channel_id=1, source_target_pairs={{8,0},{16,8},{24,16},{32,24},{40,32},{48,40},{56,48},{9,1},{17,9},... | collective-permute-start | bytes 36872 | tf_op jit(solution)/shard_map/ppermute | solution.py:22
  27.7 16.8 %collective-permute-start = (f32[3,8,128]{2,1,0:T(8,128)S(1)}, f32[3,8,128]{2,1,0:T(8,128)S(1)}, u32[]{:S(2)}, u32[]{:S(2)}) collective-permute-start(f32[3,8,128]{2,1,0:T(8,128)S(1)} %get-tuple-element.120), channel_id=1, source_target_pairs={{0,8},{8,16},{16,24},{24,32},{32,40},{40,48},{48,56},{1,9},{9,17},... | collective-permute-start | bytes 36872 | tf_op jit(solution)/shard_map/ppermute | solution.py:21
  29.8 7.6 %collective-permute-start.11 = (f32[80,8]{1,0:T(8,128)S(1)}, f32[80,8]{1,0:T(8,128)S(1)}, u32[]{:S(2)}, u32[]{:S(2)}) collective-permute-start(f32[80,8]{1,0:T(8,128)S(1)} %get-tuple-element.137), channel_id=1, source_target_pairs={{1,0},{2,1},{3,2},{4,3},{5,4},{6,5},{7,6},{9,8},{10,9},{11,10},{12... | collective-permute-start | bytes 7688 | tf_op jit(solution)/shard_map/ppermute | solution.py:22
  31.7 7.6 %collective-permute-start.10 = (f32[80,8]{1,0:T(8,128)S(1)}, f32[80,8]{1,0:T(8,128)S(1)}, u32[]{:S(2)}, u32[]{:S(2)}) collective-permute-start(f32[80,8]{1,0:T(8,128)S(1)} %get-tuple-element.136), channel_id=1, source_target_pairs={{0,1},{1,2},{2,3},{3,4},{4,5},{5,6},{6,7},{8,9},{9,10},{10,11},{11... | collective-permute-start | bytes 7688 | tf_op jit(solution)/shard_map/ppermute | solution.py:21
  37.4 5.3 %collective-permute-start.6 = (f32[80,8]{1,0:T(8,128)S(1)}, f32[80,8]{1,0:T(8,128)S(1)}, u32[]{:S(2)}, u32[]{:S(2)}) collective-permute-start(f32[80,8]{1,0:T(8,128)S(1)} %get-tuple-element.134), channel_id=1, source_target_pairs={{0,1},{1,2},{2,3},{3,4},{4,5},{5,6},{6,7},{8,9},{9,10},{10,11},{11... | collective-permute-start | bytes 7688 | tf_op jit(solution)/shard_map/ppermute | solution.py:21
  46.6 6.2 %collective-permute-start.2 = (f32[3,80,8]{2,1,0:T(8,128)S(1)}, f32[3,80,8]{2,1,0:T(8,128)S(1)}, u32[]{:S(2)}, u32[]{:S(2)}) collective-permute-start(f32[3,80,8]{2,1,0:T(8,128)S(1)} %get-tuple-element.116), channel_id=1, source_target_pairs={{0,1},{1,2},{2,3},{3,4},{4,5},{5,6},{6,7},{8,9},{9,10},{10,11},{11... | collective-permute-start | bytes 23048 | tf_op jit(solution)/shard_map/ppermute | solution.py:21
  55.3 5.9 %collective-permute-start.12 = (f32[64,128]{1,0:T(8,128)S(1)}, f32[64,128]{1,0:T(8,128)S(1)}, u32[]{:S(2)}, u32[]{:S(2)}) collective-permute-start(f32[64,128]{1,0:T(8,128)S(1)} %get-tuple-element.112), channel_id=1, source_target_pairs={{0,64},{64,128},{128,192},{192,256},{256,320},{320,384},{384,448},... | collective-permute-start | bytes 98312 | tf_op jit(solution)/shard_map/ppermute | solution.py:30
  61.2 13.7 %collective-permute-start.13 = (f32[64,128]{1,0:T(8,128)S(1)}, f32[64,128]{1,0:T(8,128)S(1)}, u32[]{:S(2)}, u32[]{:S(2)}) collective-permute-start(f32[64,128]{1,0:T(8,128)S(1)} %get-tuple-element.133), channel_id=1, source_target_pairs={{64,0},{128,64},{192,128},{256,192},{320,256},{384,320},{448,384},... | collective-permute-start | bytes 98312 | tf_op jit(solution)/shard_map/ppermute | solution.py:30
  75.0 12.1 %collective-permute-start.15 = (f32[2,4,128]{2,1,0:T(4,128)S(1)}, f32[2,4,128]{2,1,0:T(4,128)S(1)}, u32[]{:S(2)}, u32[]{:S(2)}) collective-permute-start(f32[2,4,128]{2,1,0:T(4,128)S(1)} %get-tuple-element.131), channel_id=1, source_target_pairs={{8,0},{16,8},{24,16},{32,24},{40,32},{48,40},{56,48},{9,1},{17,9},... | collective-permute-start | bytes 12296 | tf_op jit(solution)/shard_map/ppermute | solution.py:22
  84.9 11.5 %collective-permute-start.14 = (f32[2,4,128]{2,1,0:T(4,128)S(1)}, f32[2,4,128]{2,1,0:T(4,128)S(1)}, u32[]{:S(2)}, u32[]{:S(2)}) collective-permute-start(f32[2,4,128]{2,1,0:T(4,128)S(1)} %get-tuple-element.130), channel_id=1, source_target_pairs={{0,8},{8,16},{16,24},{24,32},{32,40},{40,48},{48,56},{1,9},{9,17},... | collective-permute-start | bytes 12296 | tf_op jit(solution)/shard_map/ppermute | solution.py:21
  98.5 5.7 %collective-permute-start.16 = (f32[2,72,4]{2,1,0:T(8,128)S(1)}, f32[2,72,4]{2,1,0:T(8,128)S(1)}, u32[]{:S(2)}, u32[]{:S(2)}) collective-permute-start(f32[2,72,4]{2,1,0:T(8,128)S(1)} %get-tuple-element.124), channel_id=1, source_target_pairs={{0,1},{1,2},{2,3},{3,4},{4,5},{5,6},{6,7},{8,9},{9,10},{10,11},{11... | collective-permute-start | bytes 6920 | tf_op jit(solution)/shard_map/ppermute | solution.py:21
  108.3 23.1 %all-to-all-start = ((f32[8,64,128]{2,1,0:T(8,128)}), f32[8,64,128]{2,1,0:T(8,128)S(1)}, u32[]{:S(2)}, u32[]{:S(2)}) async-start(f32[8,64,128]{2,1,0:T(8,128)} %broadcast_in_dim.19), calls=%async_computation | async-start | bytes 524288 | tf_op jit(solution)/shard_map/all_to_all | solution.py:35
  131.4 5.9 %collective-permute-start.19 = (f32[3,8,128]{2,1,0:T(8,128)S(1)}, f32[3,8,128]{2,1,0:T(8,128)S(1)}, u32[]{:S(2)}, u32[]{:S(2)}) collective-permute-start(f32[3,8,128]{2,1,0:T(8,128)S(1)} %get-tuple-element.119), channel_id=1, source_target_pairs={{8,0},{16,8},{24,16},{32,24},{40,32},{48,40},{56,48},{9,1},{17,9},... | collective-permute-start | bytes 36872 | tf_op jit(solution)/shard_map/ppermute | solution.py:22
  133.4 11.6 %collective-permute-start.18 = (f32[3,8,128]{2,1,0:T(8,128)S(1)}, f32[3,8,128]{2,1,0:T(8,128)S(1)}, u32[]{:S(2)}, u32[]{:S(2)}) collective-permute-start(f32[3,8,128]{2,1,0:T(8,128)S(1)} %get-tuple-element.118), channel_id=1, source_target_pairs={{0,8},{8,16},{16,24},{24,32},{32,40},{40,48},{48,56},{1,9},{9,17},... | collective-permute-start | bytes 36872 | tf_op jit(solution)/shard_map/ppermute | solution.py:21
  147.0 6.2 %collective-permute-start.20 = (f32[3,80,8]{2,1,0:T(8,128)S(1)}, f32[3,80,8]{2,1,0:T(8,128)S(1)}, u32[]{:S(2)}, u32[]{:S(2)}) collective-permute-start(f32[3,80,8]{2,1,0:T(8,128)S(1)} %get-tuple-element.114), channel_id=1, source_target_pairs={{0,1},{1,2},{2,3},{3,4},{4,5},{5,6},{6,7},{8,9},{9,10},{10,11},{11... | collective-permute-start | bytes 23048 | tf_op jit(solution)/shard_map/ppermute | solution.py:21
  159.8 13.7 %collective-permute-start.23 = (f32[64,128]{1,0:T(8,128)S(1)}, f32[64,128]{1,0:T(8,128)S(1)}, u32[]{:S(2)}, u32[]{:S(2)}) collective-permute-start(f32[64,128]{1,0:T(8,128)S(1)} %get-tuple-element.129), channel_id=1, source_target_pairs={{64,0},{128,64},{192,128},{256,192},{320,256},{384,320},{448,384},... | collective-permute-start | bytes 98312 | tf_op jit(solution)/shard_map/ppermute | solution.py:30
  173.6 6.1 %collective-permute-start.25 = (f32[2,4,128]{2,1,0:T(4,128)S(1)}, f32[2,4,128]{2,1,0:T(4,128)S(1)}, u32[]{:S(2)}, u32[]{:S(2)}) collective-permute-start(f32[2,4,128]{2,1,0:T(4,128)S(1)} %get-tuple-element.127), channel_id=1, source_target_pairs={{8,0},{16,8},{24,16},{32,24},{40,32},{48,40},{56,48},{9,1},{17,9},... | collective-permute-start | bytes 12296 | tf_op jit(solution)/shard_map/ppermute | solution.py:22
  175.5 11.5 %collective-permute-start.24 = (f32[2,4,128]{2,1,0:T(4,128)S(1)}, f32[2,4,128]{2,1,0:T(4,128)S(1)}, u32[]{:S(2)}, u32[]{:S(2)}) collective-permute-start(f32[2,4,128]{2,1,0:T(4,128)S(1)} %get-tuple-element.126), channel_id=1, source_target_pairs={{0,8},{8,16},{16,24},{24,32},{32,40},{40,48},{48,56},{1,9},{9,17},... | collective-permute-start | bytes 12296 | tf_op jit(solution)/shard_map/ppermute | solution.py:21
  189.0 5.7 %collective-permute-start.26 = (f32[2,72,4]{2,1,0:T(8,128)S(1)}, f32[2,72,4]{2,1,0:T(8,128)S(1)}, u32[]{:S(2)}, u32[]{:S(2)}) collective-permute-start(f32[2,72,4]{2,1,0:T(8,128)S(1)} %get-tuple-element.122), channel_id=1, source_target_pairs={{0,1},{1,2},{2,3},{3,4},{4,5},{5,6},{6,7},{8,9},{9,10},{10,11},{11... | collective-permute-start | bytes 6920 | tf_op jit(solution)/shard_map/ppermute | solution.py:21
  198.8 17.3 %all-to-all-start.1 = ((f32[8,64,128]{2,1,0:T(8,128)}), f32[8,64,128]{2,1,0:T(8,128)S(1)}, u32[]{:S(2)}, u32[]{:S(2)}) async-start(f32[8,64,128]{2,1,0:T(8,128)} %broadcast_in_dim.23), calls=%async_computation.1 | async-start | bytes 524288 | tf_op jit(solution)/shard_map/all_to_all | solution.py:35
  (12 other events, 83.9 us)
where the time goes:
time: 218 us; the launch traced here: 217 us
  starting transfers between devices  106 us (49%)
  waiting for transfers between devices  64 us (29%)
  other arithmetic  27.9 us (13%)
  local copies, waits for them, and re-layouts  17.1 us (8%)
    ppermute x12, starting transfers between devices, with_halo(): after = lax.ppermute(first, axis, down)  47.4 us
    ppermute x12, waiting for transfers between devices, with_halo(): before = lax.ppermute(last, axis, up)  41.2 us
    ppermute x12, starting transfers between devices, with_halo(): before = lax.ppermute(last, axis, up)  29.6 us
    all_to_all x2, waiting for transfers between devices, sent_to_all(): return lax.all_to_all(copies, axis, split_axis=0, concat_axis=0, tiled=True)  20 us
    all_to_all x2, starting transfers between devices, sent_to_all(): return lax.all_to_all(copies, axis, split_axis=0, concat_axis=0, tiled=True)  19.5 us
    gather x2, local copies, waits for them, and re-layouts, per_device(): predicted = final.reshape(-1)[cell_index]  12.3 us
    scatter-add x2, other arithmetic, per_device(): spread = jnp.zeros((slices_here * rows_here * cols_here,), jnp.float32).a...  11.9 us
    ppermute x4, starting transfers between devices, from_behind(): return lax.ppermute(block, axis, route)  9.33 us
  transfers between devices with their start and end apart: 30, of which 12 were waited for; matrix products, arithmetic and copies ran while one was open for 14% of the time, Pallas kernels for 0%

commit v1 on v0

v1 whole, which is shorter than its diff:
```python
import functools

import jax
import jax.numpy as jnp
from jax import lax
from jax.experimental import pallas as pl
from jax.experimental.pallas import tpu as pltpu
from jax.sharding import PartitionSpec as P

STEPS = 4
ROWS, COLS = 64, 128
EDGE = 16
HIGH = ROWS + 2 * EDGE
TALL = HIGH + 8
MID = ROWS + EDGE
BLOCK = 16
BED_RATE = 0.1
STATE_RATE = 0.5
MESH = pl.DeviceIdType.MESH

BED, S0, S1, RATE, N0, N1, V0, V1, BACK = range(9)
FIELDS = 9
STRIP = ((0, 16), (16, 16), (32, 16), (48, 16), (64, 12), (76, 12), (88, 12), (100, 12), (112, 8))
AROUND = tuple((a, b) for a in (-1, 1, 0) for b in (-1, 0, 1) if a or b)
INNER = slice(EDGE, EDGE + ROWS)


def when(cond, act):
    if cond is None:
        act()
    else:
        pl.when(cond)(act)


def rolled(value, shift):
    shift %= COLS
    return value if shift == 0 else pltpu.roll(value, shift, value.ndim - 1)


def lane(shape):
    return lax.broadcasted_iota(jnp.int32, shape, len(shape) - 1)


def ahead(main, side):
    last = lane(main.shape) == COLS - 1
    main, side = rolled(main, -1), rolled(side, -1)
    return jnp.where(last, side, main), jnp.where(last, main, side)


def behind(main, side):
    first = lane(main.shape) == 0
    main, side = rolled(main, 1), rolled(side, 1)
    return jnp.where(first, side, main), jnp.where(first, main, side)


def kernel(
    nt, nx, ny,
    states, bed, background, mask, rate, cells, values,
    states_out, bed_out,
    ff, rate_in, mask_in, cell_in, value_in, left_out, right_out, left_in, right_in,
    nxt, nxt_left, nxt_right, gain, coef, slope, path, final, adj, flux, grad,
    sums, sums_last, fin, fin_last, state1, bed1, nxt1,
    load_sem, send_sem, recv_sem,
):
    t, gx, gy = lax.axis_index("tm"), lax.axis_index("gx"), lax.axis_index("gy")

    loads = [
        pltpu.make_async_copy(src, dst, load_sem.at[i])
        for i, (src, dst) in enumerate((
            (cells, cell_in), (values, value_in), (mask, mask_in), (rate, rate_in),
            (states, ff.at[0, S0:S1 + 1, INNER]), (bed, ff.at[0, BED, INNER]),
            (background, ff.at[0, BACK, INNER]),
        ))
    ]
    for load in loads:
        load.start()

    def near(dt, dx, dy):
        parts = [None if d == 0 else (pos + d >= 0) & (pos + d < size)
                 for d, pos, size in ((dt, t, nt), (dx, gx, nx), (dy, gy, ny))]
        parts = [p for p in parts if p is not None]
        return functools.reduce(jnp.logical_and, parts), (t + dt, gx + dx, gy + dy)

    peers = [near(dt, dx, dy) for dt in (-1, 1, 0) for dx, dy in AROUND]
    peers += [(None, (lax.rem(t + d, nt), gx, gy)) for d in range(1, nt)]
    barrier = pltpu.get_barrier_semaphore()
    expected = jnp.int32(0)
    for cond, target in peers:
        when(cond, functools.partial(pl.semaphore_signal, barrier, inc=1, device_id=target, device_id_type=MESH))
        expected = expected + (1 if cond is None else cond.astype(jnp.int32))

    def clear(cond, *parts):
        def act():
            for ref, index in parts:
                ref[index] = jnp.zeros_like(ref[index])
        pl.when(cond)(act)

    for cond, rows in ((gx == 0, slice(0, EDGE)), (gx == nx - 1, slice(EDGE + ROWS, HIGH))):
        clear(cond, (ff, (0, slice(None), rows)), *((r, (rows,)) for r in (left_in, right_in, nxt, nxt_left, nxt_right)))
    clear(gy == 0, (left_in, ...), (nxt_left, ...))
    clear(gy == ny - 1, (right_in, ...), (nxt_right, ...))
    clear(t == nt - 1, (nxt, ...), (nxt_left, ...), (nxt_right, ...), (nxt1, ...))
    tail = slice(HIGH, TALL)
    for ref, index in ((ff, (slice(None), slice(0, 4), tail)), (path, (Ellipsis, tail, slice(None))),
                       (adj, (Ellipsis, tail, slice(None))), (flux, (Ellipsis, slice(0, 8), slice(None))),
                       (grad, (Ellipsis, slice(0, 8), slice(None)))):
        ref[index] = jnp.zeros_like(ref[index])

    loads[0].wait()
    loads[1].wait()
    obs = cells.shape[-1]
    for j in range(2):
        cell, value = cell_in[j, 0], value_in[j, 0]
        row, col = cell // COLS, cell % COLS
        in_row = (lax.broadcasted_iota(jnp.int32, (ROWS, obs), 0) == row).astype(jnp.float32)
        in_col = (lax.broadcasted_iota(jnp.int32, (COLS, obs), 0) == col).astype(jnp.float32).astype(jnp.bfloat16)
        parts = [in_row.astype(jnp.bfloat16)]
        rest = value
        for _ in range(3):
            part = rest.astype(jnp.bfloat16)
            rest = rest - part.astype(jnp.float32)
            parts.append((in_row * part.astype(jnp.float32)).astype(jnp.bfloat16))
        got = lax.dot_general(jnp.concatenate(parts, axis=0), in_col, (((1,), (1,)), ((), ())),
                              preferred_element_type=jnp.float32)
        ff[0, N0 + j, INNER] = got[:ROWS]
        ff[0, V0 + j, INNER] = (got[3 * ROWS:] + got[2 * ROWS:3 * ROWS]) + got[ROWS:2 * ROWS]
    loads[2].wait()
    loads[3].wait()
    ff[0, RATE, INNER] = jnp.where(mask_in[...] != 0, rate_in[...], 0.0)
    for load in loads[4:]:
        load.wait()

    for r in range(0, ROWS, BLOCK):
        at = lane((BLOCK, COLS))
        to_left = to_right = jnp.zeros((BLOCK, COLS), jnp.float32)
        for f, (start, width) in enumerate(STRIP):
            turned = rolled(ff[0, f, EDGE + r:EDGE + r + BLOCK], start)
            to_left = jnp.where((at >= start) & (at < start + width), turned, to_left)
            low = (start - width) % COLS
            if low + width <= COLS:
                here = (at >= low) & (at < low + width)
            else:
                here = (at >= low) | (at < low + width - COLS)
            to_right = jnp.where(here, turned, to_right)
        left_out[r:r + BLOCK] = to_left
        right_out[r:r + BLOCK] = to_right

    def rows_of(d):
        return {-1: (0, EDGE, EDGE + ROWS), 1: (ROWS - EDGE, EDGE, 0), 0: (0, ROWS, EDGE)}[d]

    copies = []

    def remote(cond_to, target, cond_from, src, dst):
        i = len(copies)
        copy = pltpu.make_async_remote_copy(
            src_ref=src, dst_ref=dst, send_sem=send_sem.at[i], recv_sem=recv_sem.at[i],
            device_id=target, device_id_type=MESH)
        copies.append((copy, cond_to, cond_from))
        return copies[-1]

    halo = []
    for dx, dy in AROUND:
        first, count, land = rows_of(dx)
        to, target = near(0, dx, dy)
        come, _ = near(0, -dx, -dy)
        if dy == 0:
            for fields in (slice(0, 4), slice(4, FIELDS)):
                halo.append(remote(to, target, come,
                                   ff.at[0, fields, EDGE + first:EDGE + first + count],
                                   ff.at[0, fields, land:land + count]))
        else:
            src, dst = (left_out, right_in) if dy < 0 else (right_out, left_in)
            halo.append(remote(to, target, come, src.at[first:first + count], dst.at[land:land + count]))
    for dx, dy in AROUND + ((0, 0),):
        first, count, land = rows_of(dx)
        to, target = near(-1, dx, dy)
        come, _ = near(1, -dx, -dy)
        if dy == 0:
            halo.append(remote(to, target, come, ff.at[0, S0, EDGE + first:EDGE + first + count], nxt.at[land:land + count]))
        else:
            src, dst = (left_out, nxt_right) if dy < 0 else (right_out, nxt_left)
            halo.append(remote(to, target, come, src.at[first:first + count], dst.at[land:land + count]))

    pl.semaphore_wait(barrier, expected)
    for copy, to, _ in halo:
        when(to, copy.start)
    for copy, _, come in halo:
        when(come, copy.wait_recv)

    def unpacked(f, left, right, r):
        start, width = STRIP[f]
        at = lane((BLOCK, COLS))
        from_right = rolled(right[r:r + BLOCK], -start)
        from_left = rolled(left[r:r + BLOCK], -start)
        return jnp.where(at < width, from_right, jnp.where(at >= COLS - width, from_left, 0.0))

    more = (t < nt - 1).astype(jnp.float32)
    for r in range(0, HIGH, BLOCK):
        rows = slice(r, r + BLOCK)
        for f in range(FIELDS):
            ff[1, f, rows] = unpacked(f, left_in, right_in, r)
        for p in range(2):
            following = nxt[rows] if p == 0 else unpacked(S0, nxt_left, nxt_right, r)
            gain[p, 0, rows] = ff[p, N0, rows] + 1.0
            gain[p, 1, rows] = ff[p, N1, rows] + more
            adj[p, 0, rows] = ff[p, V0, rows] + ff[p, S1, rows]
            adj[p, 1, rows] = ff[p, V1, rows] + following

    def slopes(source):
        lo, hi = source[1]
        ref = source[0]
        for r in range(lo, hi, BLOCK):
            rows = slice(r, r + BLOCK)
            main, side = ref(0, rows), ref(1, rows)
            for p, (here, up) in enumerate(zip((main, side), ahead(main, side))):
                slope[1, p, rows] = up - here
                slope[0, p, rows] = ref(p, slice(r + 1, r + 1 + BLOCK)) - here

    for r in range(0, HIGH, BLOCK):
        rows = slice(r, r + BLOCK)
        main, side = ff[0, RATE, rows], ff[1, RATE, rows]

        def mean_rate(a, b):
            return jnp.where(jnp.minimum(a, b) > 0.0, 0.5 * (a + b), 0.0)

        for p, (here, up) in enumerate(zip((main, side), ahead(main, side))):
            coef[1, p, rows] = mean_rate(here, up)
            coef[0, p, rows] = mean_rate(here, ff[p, RATE, r + 1:r + 1 + BLOCK])
    slopes((lambda p, rows: ff[p, BED, rows], (0, HIGH)))

    def faces(thick, r):
        rows = slice(r, r + BLOCK)
        here = [thick(p, rows) for p in range(2)]
        up = [[thick(p, slice(r + 1, r + 1 + BLOCK)) for p in range(2)], ahead(*here)]
        mean = [[0.5 * (here[p] + up[d][p]) for p in range(2)] for d in range(2)]
        step = [[(up[d][p] - here[p]) + slope[d, p, rows] for p in range(2)] for d in range(2)]
        return here, mean, step

    def forward(thick, out, lo, hi):
        for r in range(lo, hi, BLOCK):
            rows = slice(r, r + BLOCK)
            here, mean, step = faces(thick, r)
            f = [[coef[d, p, rows] * mean[d][p] * mean[d][p] * step[d][p] for p in range(2)] for d in range(2)]
            left = behind(*f[1])
            for p in range(2):
                flux[p, :, 8 + r:8 + r + BLOCK] = f[0][p]
                change = (f[0][p] - flux[p, :, 7 + r:7 + r + BLOCK]) + (f[1][p] - left[p])
                out(p, rows, here[p] + change)

    def backward(thick, lo, hi, begin):
        for r in range(lo, hi, BLOCK):
            rows = slice(r, r + BLOCK)
            _, mean, step = faces(thick, r)
            lam = [adj[p, :, rows] for p in range(2)]
            up = [[adj[p, :, r + 1:r + 1 + BLOCK] for p in range(2)], ahead(*lam)]
            keep, give = [[], []], [[], []]
            for d in range(2):
                for p in range(2):
                    q = coef[d, p, rows] * mean[d][p] * (lam[p] - up[d][p])
                    g, e = q * mean[d][p], q * step[d][p]
                    keep[d].append(e - g)
                    give[d].append(e + g)
                    both = g[0] + g[1]
                    spot = slice(8 + r, 8 + r + BLOCK)
                    grad[d, p, spot] = both if begin else grad[d, p, spot] + both
            given = behind(*give[1])
            for p in range(2):
                flux[p, :, 8 + r:8 + r + BLOCK] = give[0][p]
                adj[p, :, rows] = lam[p] + (keep[0][p] + flux[p, :, 7 + r:7 + r + BLOCK]) + (keep[1][p] + given[p])

    def bed_gradient(r, count):
        spot, before = slice(8 + r, 8 + r + count), slice(7 + r, 7 + r + count)
        left = behind(grad[1, 0, spot], grad[1, 1, spot])
        return [(grad[0, p, before] - grad[0, p, spot]) + (left[p] - grad[1, p, spot]) for p in range(2)]

    def at_step(k, start):
        return start if k == 0 else (lambda p, rows: path[k - 1, p, :, rows])

    def run(start, which, lo, hi, weights):
        def store(k):
            def put(p, rows, value):
                if k < STEPS:
                    path[k - 1, p, :, rows] = value
                else:
                    final[which, p, :, rows] = value
                    adj[p, :, rows] = weights(p, rows) * value - adj[p, :, rows]
            return put

        for k in range(STEPS):
            forward(at_step(k, start), store(k + 1), lo, hi)

    def pull(start, lo, hi):
        for k in reversed(range(STEPS)):
            backward(at_step(k, start), lo, hi, k == STEPS - 1)

    def weights(p, rows):
        return gain[p, :, rows]

    def broadcast(buffer):
        out = []
        for d in sorted(range(1, nt), key=lambda d: -min(d, nt - d)):
            out.append((remote(None, (lax.rem(t + d, nt), gx, gy), None, buffer.at[t], buffer.at[t]), d))
        for (copy, _, _), _ in out:
            copy.start()
        return [(copy, buffer.at[lax.rem(t + nt - d, nt)]) for (copy, _, _), d in out]

    def arrived(sent):
        for copy, _ in sent:
            copy.wait_recv()

    before, after = near(-1, 0, 0), near(1, 0, 0)
    lo, hi = (HIGH - MID) // 2, (HIGH + MID) // 2
    at = lane((8, COLS))

    def first(p, rows):
        return ff[p, S0:S1 + 1, rows]

    run(first, 0, 0, HIGH, weights)
    fin_copy = remote(after[0], after[1], before[0], final.at[0, :, 1, lo:hi], fin)
    when(after[0], fin_copy[0].start)
    pull(first, 0, HIGH)
    packed = [jnp.zeros((8, COLS), jnp.float32)] * 2
    for k in range(MID // 8):
        main, side = bed_gradient(lo + 8 * k, 8)
        sums[t, 8 * k:8 * k + 8] = main
        turned = rolled(side, 16 * k)
        slot = 16 * (k % 8)
        here = (at >= slot - 8) & (at < slot + 8) if slot else (at < 8) | (at >= COLS - 8)
        packed[k // 8] = jnp.where(here, turned, packed[k // 8])
    sums[t, MID:MID + 8] = packed[0]
    sums[t, MID + 8:MID + 16] = packed[1]
    sent = broadcast(sums)

    when(before[0], fin_copy[0].wait_recv)
    for r in range(lo, hi, BLOCK):
        rows, short = slice(r, r + BLOCK), slice(r - lo, r - lo + BLOCK)
        for p in range(2):
            begun = jnp.where(t == 0, ff[p, BACK, rows], fin[p, short])
            s0, s1 = ff[p, S0, rows], ff[p, S1, rows]
            state1[p, 0, rows] = s0 - STATE_RATE * ((s0 - begun) + adj[p, 0, rows])
            state1[p, 1, rows] = s1 - STATE_RATE * ((s1 - final[0, p, 0, rows]) + adj[p, 1, rows])
    nxt_copy = remote(before[0], before[1], after[0], state1.at[:, 0, lo:hi], nxt1)
    when(before[0], nxt_copy[0].start)

    arrived(sent)

    def total(ref, rows):
        got = ref[0, rows]
        for i in range(1, nt):
            got = got + ref[i, rows]
        return got

    sides = [total(sums, slice(MID + 8 * i, MID + 8 * i + 8)) for i in range(2)]
    for k in range(MID // 8):
        rows = slice(lo + 8 * k, lo + 8 * k + 8)
        main = total(sums, slice(8 * k, 8 * k + 8))
        side = jnp.where((at < 8) | (at >= COLS - 8), rolled(sides[k // 8], -16 * k), 0.0)
        for p, got in enumerate((main, side)):
            bed1[p, rows] = ff[p, BED, rows] - BED_RATE * got

    bed1[:, hi:hi + 8] = jnp.zeros((2, 8, COLS), jnp.float32)
    state1[:, :, hi:hi + 8] = jnp.zeros((2, 2, 8, COLS), jnp.float32)

    def second(p, rows):
        return state1[p, :, rows]

    slopes((lambda p, rows: bed1[p, rows], (lo, hi)))
    for k in range(STEPS - 1):
        forward(at_step(k, second), lambda p, rows, value, k=k: path.__setitem__((k, p, slice(None), rows), value), lo, hi)
    when(after[0], nxt_copy[0].wait_recv)
    for r in range(lo, hi, BLOCK):
        rows, short = slice(r, r + BLOCK), slice(r - lo, r - lo + BLOCK)
        for p in range(2):
            adj[p, 0, rows] = ff[p, V0, rows] + state1[p, 1, rows]
            adj[p, 1, rows] = ff[p, V1, rows] + nxt1[p, short]

    def last(p, rows, value):
        final[1, p, :, rows] = value
        adj[p, :, rows] = weights(p, rows) * value - adj[p, :, rows]

    forward(at_step(STEPS - 1, second), last, lo, hi)
    fin_last_copy = remote(after[0], after[1], before[0], final.at[1, 0, 1, INNER], fin_last)
    when(after[0], fin_last_copy[0].start)
    pull(second, lo, hi)
    for r in range(EDGE, EDGE + ROWS, BLOCK):
        sums_last[t, r - EDGE:r - EDGE + BLOCK] = bed_gradient(r, BLOCK)[0]
    sent_last = broadcast(sums_last)

    when(before[0], fin_last_copy[0].wait_recv)
    for r in range(0, ROWS, BLOCK):
        rows, short = slice(EDGE + r, EDGE + r + BLOCK), slice(r, r + BLOCK)
        begun = jnp.where(t == 0, ff[0, BACK, rows], fin_last[short])
        s0, s1 = state1[0, 0, rows], state1[0, 1, rows]
        states_out[0, short] = s0 - STATE_RATE * ((s0 - begun) + adj[0, 0, rows])
        states_out[1, short] = s1 - STATE_RATE * ((s1 - final[1, 0, 0, rows]) + adj[0, 1, rows])
    arrived(sent_last)
    for r in range(0, ROWS, BLOCK):
        rows, short = slice(EDGE + r, EDGE + r + BLOCK), slice(r, r + BLOCK)
        now = bed1[0, rows]
        bed_out[short] = now - BED_RATE * (total(sums_last, short) + (now - ff[0, BED, rows]))
    for copy, to, _ in copies:
        when(to, copy.wait_send)


def solution(mesh):
    nt, nx, ny = (mesh.shape[a] for a in ("tm", "gx", "gy"))
    f32 = jnp.float32

    def step(states, bed, background, mask, rate, cells, values):
        obs = cells.shape[-1]
        count = 19 + 2 * (nt - 1) + 3
        vmem = pltpu.VMEM
        return pl.pallas_call(
            functools.partial(kernel, nt, nx, ny),
            out_shape=(jax.ShapeDtypeStruct(states.shape, f32), jax.ShapeDtypeStruct(bed.shape, f32)),
            in_specs=[pl.BlockSpec(memory_space=pl.ANY)] * 7,
            out_specs=(pl.BlockSpec(memory_space=vmem),) * 2,
            scratch_shapes=[
                vmem((2, FIELDS, TALL, COLS), f32),
                vmem((ROWS, COLS), f32), vmem((ROWS, COLS), jnp.int32),
                vmem((2, 1, 1, obs), jnp.int32), vmem((2, 1, 1, obs), f32),
                vmem((ROWS, COLS), f32), vmem((ROWS, COLS), f32),
                vmem((HIGH, COLS), f32), vmem((HIGH, COLS), f32),
                vmem((HIGH, COLS), f32), vmem((HIGH, COLS), f32), vmem((HIGH, COLS), f32),
                vmem((2, 2, HIGH, COLS), f32),
                vmem((2, 2, HIGH, COLS), f32), vmem((2, 2, HIGH, COLS), f32),
                vmem((STEPS - 1, 2, 2, TALL, COLS), f32),
                vmem((2, 2, 2, HIGH, COLS), f32),
                vmem((2, 2, TALL, COLS), f32),
                vmem((2, 2, 8 + HIGH, COLS), f32), vmem((2, 2, 8 + HIGH, COLS), f32),
                vmem((nt, MID + 16, COLS), f32), vmem((nt, ROWS, COLS), f32),
                vmem((2, MID, COLS), f32), vmem((ROWS, COLS), f32),
                vmem((2, 2, HIGH, COLS), f32), vmem((2, HIGH, COLS), f32),
                vmem((2, MID, COLS), f32),
                pltpu.SemaphoreType.DMA((7,)),
                pltpu.SemaphoreType.DMA((count,)), pltpu.SemaphoreType.DMA((count,)),
            ],
            compiler_params=pltpu.CompilerParams(
                collective_id=0, has_side_effects=True, vmem_limit_bytes=32 << 20),
            name="assimilate",
        )(states, bed, background, mask, rate, cells, values)

    return jax.shard_map(
        step,
        mesh=mesh,
        in_specs=(P("tm", "gx", "gy"),) + (P("gx", "gy"),) * 4 + (P("tm", "gx", "gy", None),) * 2,
        out_specs=(P("tm", "gx", "gy"), P("gx", "gy")),
        check_vma=False,
    )
```

time: 218 us -> 56.1 us (0.26)
  the two profiles are of different devices: /device:TPU:56 before, /device:TPU:48 now
where the time goes in v1:
time: 56.1 us; the launch traced here: 55.6 us
  Pallas kernels  48.5 us (86%)
  local copies, waits for them, and re-layouts  6.48 us (12%)
  between operations  0.66 us (1%)
    pallas_call x1, Pallas kernels, step(): pl.pallas_call(functools.partial(kernel, nt, nx, ny), out_shape=(jax.Shap...  48.5 us
    unnamed x16, local copies, waits for them, and re-layouts  6.48 us

profile of v1, /device:TPU:48, one launch (start us, length us, event | category | flops | bytes accessed | tf_op | source)
XLA Modules:
  0.0 55.6 jit_solution(15746256170365119393)
XLA Ops:
  0.6 0.0 copy-start
  0.6 0.8 %copy-done = f32[2,64,128]{2,1,0:T(8,128)S(1)} copy-done((f32[2,64,128]{2,1,0:T(8,128)S(1)}, f32[2,64,128]{2,1,0:T(8,128)}, u32[]{:S(2)}) %copy-start) | copy-done | bytes 65560
  1.5 0.0 copy-start.1
  1.5 0.8 %copy-done.1 = f32[64,128]{1,0:T(8,128)S(1)} copy-done((f32[64,128]{1,0:T(8,128)S(1)}, f32[64,128]{1,0:T(8,128)}, u32[]{:S(2)}) %copy-start.1) | copy-done | bytes 32792
  2.2 0.0 copy-start.2
  2.2 0.8 %copy-done.2 = f32[64,128]{1,0:T(8,128)S(1)} copy-done((f32[64,128]{1,0:T(8,128)S(1)}, f32[64,128]{1,0:T(8,128)}, u32[]{:S(2)}) %copy-start.2) | copy-done | bytes 32792
  3.0 0.0 copy-start.3
  3.0 0.8 %copy-done.3 = s32[64,128]{1,0:T(8,128)S(1)} copy-done((s32[64,128]{1,0:T(8,128)S(1)}, s32[64,128]{1,0:T(8,128)}, u32[]{:S(2)}) %copy-start.3) | copy-done | bytes 32792
  3.7 0.0 copy-start.4
  3.8 0.8 %copy-done.4 = f32[64,128]{1,0:T(8,128)S(1)} copy-done((f32[64,128]{1,0:T(8,128)S(1)}, f32[64,128]{1,0:T(8,128)}, u32[]{:S(2)}) %copy-start.4) | copy-done | bytes 32792
  4.5 0.0 copy-start.5
  4.5 0.7 %copy-done.5 = s32[2,1,1,512]{3,2,1,0:T(1,128)S(1)} copy-done((s32[2,1,1,512]{3,2,1,0:T(1,128)S(1)}, s32[2,1,1,512]{3,2,1,0:T(1,128)}, u32[]{:S(2)}) %copy-start.5) | copy-done | bytes 4120
  5.2 0.0 copy-start.6
  5.2 0.7 %copy-done.6 = f32[2,1,1,512]{3,2,1,0:T(1,128)S(1)} copy-done((f32[2,1,1,512]{3,2,1,0:T(1,128)S(1)}, f32[2,1,1,512]{3,2,1,0:T(1,128)}, u32[]{:S(2)}) %copy-start.6) | copy-done | bytes 4120
  5.9 48.5 %assimilate.1 = (f32[2,64,128]{2,1,0:T(8,128)S(1)}, f32[64,128]{1,0:T(8,128)S(1)}) custom-call(f32[2,64,128]{2,1,0:T(8,128)S(1)} %copy-done, f32[64,128]{1,0:T(8,128)S(1)} %copy-done.1, f32[64,128]{1,0:T(8,128)S(1)} %copy-done.2, s32[64,128]{1,0:T(8,128)S(1)} %copy-done.3, f32[64,128]{1,0:T(8,128)S(1)} %copy-done.4, s32[2,1,1,512]{3,2,1,0:T(1,128)S(1)} %copy-done.5, ...), custom_call_target="tpu_custom_call" | custom-call | tf_op jit(solution)/shard_map/assimilate/pallas_call | solution.py:413
  54.4 0.6 %copy.11 = f32[2,64,128]{2,1,0:T(8,128)} copy(f32[2,64,128]{2,1,0:T(8,128)S(1)} %get-tuple-element.4) | data formatting | bytes 131072
  55.0 0.6 %copy.12 = f32[64,128]{1,0:T(8,128)} copy(f32[64,128]{1,0:T(8,128)S(1)} %get-tuple-element.5) | data formatting | bytes 65536
Async XLA Ops:
  0.6 0.8 %copy-start = (f32[2,64,128]{2,1,0:T(8,128)S(1)}, f32[2,64,128]{2,1,0:T(8,128)}, u32[]{:S(2)}) copy-start(f32[2,64,128]{2,1,0:T(8,128)} %states.1) | copy-start | bytes 196612
  1.5 0.8 %copy-start.1 = (f32[64,128]{1,0:T(8,128)S(1)}, f32[64,128]{1,0:T(8,128)}, u32[]{:S(2)}) copy-start(f32[64,128]{1,0:T(8,128)} %bed.1) | copy-start | bytes 98308
  2.2 0.8 %copy-start.2 = (f32[64,128]{1,0:T(8,128)S(1)}, f32[64,128]{1,0:T(8,128)}, u32[]{:S(2)}) copy-start(f32[64,128]{1,0:T(8,128)} %background.1) | copy-start | bytes 98308
  3.0 0.8 %copy-start.3 = (s32[64,128]{1,0:T(8,128)S(1)}, s32[64,128]{1,0:T(8,128)}, u32[]{:S(2)}) copy-start(s32[64,128]{1,0:T(8,128)} %mask.1) | copy-start | bytes 98308
  3.7 0.8 %copy-start.4 = (f32[64,128]{1,0:T(8,128)S(1)}, f32[64,128]{1,0:T(8,128)}, u32[]{:S(2)}) copy-start(f32[64,128]{1,0:T(8,128)} %rate.1) | copy-start | bytes 98308
  4.5 0.7 %copy-start.5 = (s32[2,1,1,512]{3,2,1,0:T(1,128)S(1)}, s32[2,1,1,512]{3,2,1,0:T(1,128)}, u32[]{:S(2)}) copy-start(s32[2,1,1,512]{3,2,1,0:T(1,128)} %cells.1) | copy-start | bytes 12292
  5.2 0.7 %copy-start.6 = (f32[2,1,1,512]{3,2,1,0:T(1,128)S(1)}, f32[2,1,1,512]{3,2,1,0:T(1,128)}, u32[]{:S(2)}) copy-start(f32[2,1,1,512]{3,2,1,0:T(1,128)} %values.1) | copy-start | bytes 12292

commit v2 on v0

v2 whole, which is shorter than its diff:
```python
import functools

import jax
import jax.numpy as jnp
from jax import lax
from jax.experimental import pallas as pl
from jax.experimental.pallas import tpu as pltpu
from jax.sharding import PartitionSpec as P

STEPS = 4
ROWS, COLS = 64, 128
EDGE = 16
HIGH = ROWS + 2 * EDGE
MID = ROWS + EDGE
END = 2 * EDGE
BLOCK = 16
BED_RATE = 0.1
STATE_RATE = 0.5
MESH = pl.DeviceIdType.MESH

BED, S0, S1, RATE, N0, N1, V0, V1, BACK = range(9)
FIELDS = 9
STRIP = ((0, 16), (16, 16), (32, 16), (48, 16), (64, 12), (76, 12), (88, 12), (100, 12), (112, 8))
CORNERS = ((1, -1), (1, 1), (-1, -1), (-1, 1))
AROUND = ((1, 0), (-1, 0)) + CORNERS + ((0, -1), (0, 1))


def when(cond, act):
    if cond is None:
        act()
    else:
        pl.when(cond)(act)


def span(start, size):
    return pl.ds(pl.multiple_of(start, 8), size)


def rolled(value, shift):
    shift %= COLS
    return value if shift == 0 else pltpu.roll(value, shift, value.ndim - 1)


def lane(shape):
    return lax.broadcasted_iota(jnp.int32, shape, len(shape) - 1)


def ahead(main, side):
    last = lane(main.shape) == COLS - 1
    main, side = rolled(main, -1), rolled(side, -1)
    return jnp.where(last, side, main), jnp.where(last, main, side)


def behind(main, side):
    first = lane(main.shape) == 0
    main, side = rolled(main, 1), rolled(side, 1)
    return jnp.where(first, side, main), jnp.where(first, main, side)


def within(at, start, width):
    start %= COLS
    if start + width <= COLS:
        return (at >= start) & (at < start + width)
    return (at >= start) | (at < start + width - COLS)


def counted(cell, value, rows, skip):
    obs = cell.shape[-1]
    row, col = cell // COLS - skip, cell % COLS
    in_row = (lax.broadcasted_iota(jnp.int32, (rows, obs), 0) == row).astype(jnp.float32)
    in_col = (lax.broadcasted_iota(jnp.int32, (COLS, obs), 0) == col).astype(jnp.float32).astype(jnp.bfloat16)
    parts = [in_row.astype(jnp.bfloat16)]
    rest = value
    for _ in range(3):
        part = rest.astype(jnp.bfloat16)
        rest = rest - part.astype(jnp.float32)
        parts.append((in_row * part.astype(jnp.float32)).astype(jnp.bfloat16))
    got = lax.dot_general(jnp.concatenate(parts, axis=0), in_col, (((1,), (1,)), ((), ())),
                          preferred_element_type=jnp.float32)
    return got[:rows], (got[3 * rows:] + got[2 * rows:3 * rows]) + got[rows:2 * rows]


class Model:
    def __init__(self, rows, field, coef, slope, path, adj, flux, grad, gain, final):
        self.rows, self.field, self.coef, self.slope, self.path = rows, field, coef, slope, path
        self.adj, self.flux, self.grad, self.gain, self.final = adj, flux, grad, gain, final

    def blocks(self):
        return [slice(r, r + BLOCK) for r in range(0, self.rows, BLOCK)]

    def clear_ends(self):
        tail = slice(self.rows, self.rows + 8)
        for ref, index in ((self.field, (Ellipsis, tail, slice(None))), (self.path, (Ellipsis, tail, slice(None))),
                           (self.adj, (Ellipsis, tail, slice(None))), (self.flux, (Ellipsis, slice(0, 8), slice(None))),
                           (self.grad, (Ellipsis, slice(0, 8), slice(None)))):
            ref[index] = jnp.zeros_like(ref[index])

    def coefficients(self):
        def mean_rate(a, b):
            return jnp.where(jnp.minimum(a, b) > 0.0, 0.5 * (a + b), 0.0)

        for rows in self.blocks():
            both = [self.field[p, RATE, rows] for p in range(2)]
            for p, (here, up) in enumerate(zip(both, ahead(*both))):
                self.coef[1, p, rows] = mean_rate(here, up)
                self.coef[0, p, rows] = mean_rate(here, self.field[p, RATE, rows.start + 1:rows.stop + 1])

    def slopes(self):
        for rows in self.blocks():
            both = [self.field[p, BED, rows] for p in range(2)]
            for p, (here, up) in enumerate(zip(both, ahead(*both))):
                self.slope[1, p, rows] = up - here
                self.slope[0, p, rows] = self.field[p, BED, rows.start + 1:rows.stop + 1] - here

    def thick(self, k, p, rows):
        return self.field[p, S0:S1 + 1, rows] if k == 0 else self.path[k - 1, p, :, rows]

    def faces(self, k, rows):
        here = [self.thick(k, p, rows) for p in range(2)]
        up = [[self.thick(k, p, slice(rows.start + 1, rows.stop + 1)) for p in range(2)], ahead(*here)]
        mean = [[0.5 * (here[p] + up[d][p]) for p in range(2)] for d in range(2)]
        step = [[(up[d][p] - here[p]) + self.slope[d, p, rows] for p in range(2)] for d in range(2)]
        return here, mean, step

    def forward(self, k):
        for rows in self.blocks():
            here, mean, step = self.faces(k, rows)
            f = [[self.coef[d, p, rows] * mean[d][p] * mean[d][p] * step[d][p] for p in range(2)] for d in range(2)]
            left = behind(*f[1])
            for p in range(2):
                self.flux[p, :, 8 + rows.start:8 + rows.stop] = f[0][p]
                new = here[p] + ((f[0][p] - self.flux[p, :, 7 + rows.start:7 + rows.stop]) + (f[1][p] - left[p]))
                if k + 1 < STEPS:
                    self.path[k, p, :, rows] = new
                else:
                    self.final[p, :, rows] = new

    def force(self):
        for rows in self.blocks():
            for p in range(2):
                self.adj[p, :, rows] = self.gain[p, :, rows] * self.final[p, :, rows] - self.adj[p, :, rows]

    def backward(self, k):
        for rows in self.blocks():
            _, mean, step = self.faces(k, rows)
            lam = [self.adj[p, :, rows] for p in range(2)]
            up = [[self.adj[p, :, rows.start + 1:rows.stop + 1] for p in range(2)], ahead(*lam)]
            spot = slice(8 + rows.start, 8 + rows.stop)
            keep, give = [[], []], [[], []]
            for d in range(2):
                for p in range(2):
                    q = self.coef[d, p, rows] * mean[d][p] * (lam[p] - up[d][p])
                    g, e = q * mean[d][p], q * step[d][p]
                    keep[d].append(e - g)
                    give[d].append(e + g)
                    both = g[0] + g[1]
                    self.grad[d, p, spot] = both if k == STEPS - 1 else self.grad[d, p, spot] + both
            given = behind(*give[1])
            for p in range(2):
                self.flux[p, :, spot] = give[0][p]
                self.adj[p, :, rows] = (
                    lam[p] + (keep[0][p] + self.flux[p, :, 7 + rows.start:7 + rows.stop]) + (keep[1][p] + given[p]))

    def pull(self):
        for k in reversed(range(STEPS)):
            self.backward(k)

    def bed_gradient(self, r, count):
        spot, before = slice(8 + r, 8 + r + count), slice(7 + r, 7 + r + count)
        left = behind(self.grad[1, 0, spot], self.grad[1, 1, spot])
        return [(self.grad[0, p, before] - self.grad[0, p, spot]) + (left[p] - self.grad[1, p, spot]) for p in range(2)]


def kernel(
    nt, nx, ny,
    states, bed, background, mask, rate, cells, values,
    states_out, bed_out,
    ff, rate_in, mask_in, cell_in, value_in, cell_near, value_near, left_out, right_out, left_in, right_in,
    nxt, fold_out, fold_in, foll1, foll2,
    field1, coef1, slope1, path1, adj1, flux1, grad1, gain1, final1,
    field2, coef2, slope2, path2, adj2, flux2, grad2, gain2, final2,
    field3, gain3, final3, final4,
    pull1, pull2, pull3, back1, back2,
    mine, theirs, pairs, sums2, sums3, sums4, fin_out1, fin_out2, fin1, fin2, fin_last, lam_out1, lam_out2, lam1, lam2,
    load_sem, send_sem, recv_sem,
):
    t, gx, gy = lax.axis_index("tm"), lax.axis_index("gx"), lax.axis_index("gy")
    half = nx // 2
    low = gx < half
    high = jnp.logical_not(low)

    def place(side, is_low):
        return jnp.where(is_low, *{-1: (0, MID), 0: (EDGE, 0), 1: (MID, ROWS)}[side])

    home = place(0, low)
    inner = span(home, ROWS)

    loads = [
        pltpu.make_async_copy(src, dst, load_sem.at[i])
        for i, (src, dst) in enumerate((
            (cells, cell_in), (values, value_in), (mask, mask_in), (rate, rate_in),
            (states, ff.at[S0:S1 + 1, inner]), (bed, ff.at[BED, inner]), (background, ff.at[BACK, inner]),
        ))
    ]
    for load in loads:
        load.start()

    def near(dt, dx, dy):
        parts = [None if d == 0 else (pos + d >= 0) & (pos + d < size)
                 for d, pos, size in ((dt, t, nt), (dx, gx, nx), (dy, gy, ny))]
        parts = [p for p in parts if p is not None]
        return functools.reduce(jnp.logical_and, parts), (t + dt, gx + dx, gy + dy)

    def middle(dx):
        return low != (gx + dx < half)

    def both(*conds):
        conds = [c for c in conds if c is not None]
        return functools.reduce(jnp.logical_and, conds) if conds else None

    peers = []
    for dt in (0, -1, 1):
        for dx, dy in AROUND:
            cond, target = near(dt, dx, dy)
            peers.append((both(cond, jnp.logical_not(middle(dx))) if dt and dx else cond, target))
    peers += [(None, (lax.rem(t + d, nt), gx, gy)) for d in range(1, nt)]
    barrier = pltpu.get_barrier_semaphore()
    expected = jnp.int32(0)
    for cond, target in peers:
        when(cond, functools.partial(pl.semaphore_signal, barrier, inc=1, device_id=target, device_id_type=MESH))
        expected = expected + (1 if cond is None else cond.astype(jnp.int32))

    def clear(cond, *parts):
        def act():
            for ref, index in parts:
                ref[index] = jnp.zeros_like(ref[index])
        pl.when(cond)(act)

    side_rows = slice(None)
    for cond, rows, side in ((gx == 0, slice(0, EDGE), 0), (gx == nx - 1, slice(ROWS, MID), 1)):
        clear(cond, (ff, (side_rows, rows)), (left_in, rows), (right_in, rows), (nxt, rows),
              (fold_in, (slice(None), 2 * side)), (value_near, side))
        pl.when(cond)(functools.partial(
            cell_near.__setitem__, side, jnp.full(cell_near.shape[1:], -1, jnp.int32)))
    clear(gy == 0, (left_in, ...), (fold_in, 0))
    clear(gy == ny - 1, (right_in, ...), (fold_in, 1))
    clear(t == nt - 1, (nxt, ...), (fold_in, ...))

    one = Model(MID, field1, coef1, slope1, path1, adj1, flux1, grad1, gain1, final1)
    two = Model(END, field2, coef2, slope2, path2, adj2, flux2, grad2, gain2, final2)
    again = Model(ROWS, field3, coef1, slope1, path1, adj1, flux1, grad1, gain3, final3)
    rest = Model(END, field2, coef2, slope2, path2, adj2, flux2, grad2, gain2, final4)
    for part in (one, two):
        part.clear_ends()

    loads[0].wait()
    loads[1].wait()
    for j in range(2):
        ff[N0 + j, inner], ff[V0 + j, inner] = counted(cell_in[j, 0], value_in[j, 0], ROWS, 0)
    loads[2].wait()
    loads[3].wait()
    ff[RATE, inner] = jnp.where(mask_in[...] != 0, rate_in[...], 0.0)
    for load in loads[4:]:
        load.wait()

    at = lane((BLOCK, COLS))
    at8 = lane((8, COLS))
    for r in range(0, ROWS, BLOCK):
        to_left = to_right = jnp.zeros((BLOCK, COLS), jnp.float32)
        for f, (start, width) in enumerate(STRIP):
            turned = rolled(ff[f, span(home + r, BLOCK)], start)
            to_left = jnp.where(within(at, start, width), turned, to_left)
            to_right = jnp.where(within(at, start - width, width), turned, to_right)
        left_out[r:r + BLOCK] = to_left
        right_out[r:r + BLOCK] = to_right

    def fold(to, field):
        to_left = to_right = jnp.zeros((8, COLS), jnp.float32)
        for k in range(ROWS // 8):
            turned = rolled(field[span(home + 8 * k, 8)], 16 * k)
            to_left = jnp.where(within(at8, 16 * k, 16), turned, to_left)
            to_right = jnp.where(within(at8, 16 * k - 16, 16), turned, to_right)
        fold_out[to, 0], fold_out[to, 1] = to_left, to_right

    fold(0, ff.at[S0])

    def first_row(dx):
        return ROWS - EDGE if dx > 0 else 0

    copies = []

    def remote(to, target, src, dst):
        i = len(copies)
        copy = pltpu.make_async_remote_copy(
            src_ref=src, dst_ref=dst, send_sem=send_sem.at[i], recv_sem=recv_sem.at[i],
            device_id=target, device_id_type=MESH)
        copies.append((copy, to))
        return copy

    def halo(dt, dx, dy, pick, also_to=None, also_from=None):
        to, target = near(dt, dx, dy)
        come, _ = near(-dt, -dx, -dy)
        to, come = both(to, also_to), both(come, also_from)
        count = EDGE if dx else ROWS
        land = span(place(-dx, gx + dx < half), count)
        return remote(to, target, *pick(span(home + first_row(dx), count), pl.ds(first_row(dx), count), land)), to, come, dx

    def strips(dy):
        out, into = (left_out, right_in) if dy < 0 else (right_out, left_in)
        return lambda own, tile, land: (out.at[tile], into.at[land])

    early = [halo(0, dx, 0, lambda own, tile, land: (ff.at[0:4, own], ff.at[0:4, land])) for dx in (1, -1)]
    early += [halo(0, dx, dy, strips(dy)) for dx, dy in CORNERS + ((0, -1), (0, 1))]
    late = []
    for dx in (1, -1):
        side = 0 if dx > 0 else 1
        late.append(halo(0, dx, 0, lambda own, tile, land: (cell_in, cell_near.at[side])))
        late.append(halo(0, dx, 0, lambda own, tile, land: (value_in, value_near.at[side])))
    def next_slice(i, field, dx, dy):
        if dy == 0:
            return lambda own, tile, land: (field.at[own], nxt.at[land])
        return lambda own, tile, land: (fold_out.at[i, 0 if dy < 0 else 1], fold_in.at[1 if dy < 0 else 0, 1 - dx])

    next_tile = halo(-1, 0, 0, next_slice(0, ff.at[S0], 0, 0))
    for dx, dy in AROUND:
        conds = [None] * 2 if dx == 0 else [jnp.logical_not(middle(d)) for d in (dx, -dx)]
        late.append(halo(-1, dx, dy, next_slice(0, ff.at[S0], dx, dy), *conds))
    for dx in (1, -1):
        late.append(halo(0, dx, 0, lambda own, tile, land: (ff.at[BACK, own], ff.at[BACK, land]), t == 0, t == 0))
    onward = [halo(0, dx, dy, next_slice(1, nxt, dx, dy), *(both(t < nt - 1, middle(d)) for d in (dx, -dx)))
              for dx, dy in AROUND if dx]

    pl.semaphore_wait(barrier, expected)
    for copy, to, _, _ in [next_tile] + early + late:
        when(to, copy.start)
    when(next_tile[2], next_tile[0].wait_recv)

    @pl.when((t < nt - 1) & (middle(1) | middle(-1)))
    def _():
        fold(1, nxt)

    for copy, to, _, _ in onward:
        when(to, copy.start)
    late += onward

    def arrive(group, far):
        for copy, _, come, dx in group:
            if dx:
                when(come & (low if (dx > 0) != far else high), copy.wait_recv)
            elif not far:
                when(come, copy.wait_recv)

    def unpacked(f, rows):
        start, width = STRIP[f]
        return jnp.where(at < width, rolled(right_in[rows], -start),
                         jnp.where(at >= COLS - width, rolled(left_in[rows], -start), 0.0))

    def take(part, r, rows):
        to = slice(r, r + BLOCK)
        for f in range(4):
            part.field[0, f, to] = ff[f, rows]
            part.field[1, f, to] = unpacked(f, rows)

    def unfolded(spots):
        out = []
        for pair in spots:
            which = jnp.where(low, pair[0][0], pair[1][0])
            left, right = fold_in[0, which], fold_in[1, which]
            got = [jnp.where(at8 < 16, rolled(right, -16 * k), jnp.where(at8 >= COLS - 16, rolled(left, -16 * k), 0.0))
                   for _, k in pair]
            out.append(jnp.where(low, *got))
        return jnp.concatenate(out, axis=0)

    more = (t < nt - 1).astype(jnp.float32)

    def demand(part, pulls, back, foll, r, rows, spots):
        to = slice(r, r + BLOCK)
        back[0, to], back[1, to] = ff[BACK, rows], unpacked(BACK, rows)
        for p in range(2):
            got = [ff[f, rows] if p == 0 else unpacked(f, rows) for f in (N0, N1, V0, V1)]
            following = nxt[rows] if p == 0 else unfolded(spots)
            foll[p, to] = following
            part.gain[p, 0, to], part.gain[p, 1, to] = got[0] + 1.0, got[1] + more
            pulls[p, 0, to], pulls[p, 1, to] = got[2], got[3]
            part.adj[p, 0, to] = got[2] + part.field[p, S1, to]
            part.adj[p, 1, to] = got[3] + following

    def beside(far):
        from_up = low if not far else high
        side, skip = jnp.where(from_up, 0, 1), jnp.where(from_up, ROWS - EDGE, 0)
        rows = span(MID if far else jnp.where(low, 0, ROWS), EDGE)
        for j in range(2):
            ff[N0 + j, rows], ff[V0 + j, rows] = counted(cell_near[side, j, 0], value_near[side, j, 0], EDGE, skip)

    arrive(early, False)
    for r in range(0, MID, BLOCK):
        take(one, r, slice(r, r + BLOCK))
    one.coefficients()
    one.slopes()
    for k in range(STEPS):
        one.forward(k)
    before, after = near(-1, 0, 0), near(1, 0, 0)

    def pack(to, groups, get):
        packed = jnp.zeros((8, COLS), jnp.float32)
        for k in range(groups):
            main, side = get(8 + 8 * k)
            to[8 * k:8 * k + 8] = main
            packed = jnp.where(within(at8, 16 * k - 8, 16), rolled(side, 16 * k), packed)
        to[8 * groups:8 * groups + 8] = packed

    def unpack(ref, groups, k):
        side = rolled(ref[8 * groups:8 * groups + 8], -16 * k)
        return ref[8 * k:8 * k + 8], jnp.where(within(at8, -8, 16), side, 0.0)

    def send_final(part, to, into):
        pack(to, (part.rows - 16) // 8, lambda r: [part.final[p, 1, r:r + 8] for p in range(2)])
        copy = remote(*after, to, into)
        when(after[0], copy.start)
        return copy

    def send_adjoint(part, to, into):
        pack(to, (part.rows - 16) // 8, lambda r: [part.adj[p, 0, r:r + 8] for p in range(2)])
        copy = remote(*before, to, into)
        when(before[0], copy.start)
        return copy

    fin_copies = [send_final(one, fin_out1, fin1)]
    arrive(late, False)
    beside(False)
    for r in range(0, MID, BLOCK):
        spots = []
        for g in (r // 8, r // 8 + 1):
            spots.append([(0, 6 + g) if g < 2 else (1, g - 2), (1, g) if g < 8 else (2, g - 8)])
        demand(one, pull1, back1, foll1, r, slice(r, r + BLOCK), spots)
    one.force()

    dest1, dest2 = jnp.where(low, 0, EDGE), jnp.where(low, ROWS, 0)
    one.pull()

    def broadcast(buffer):
        out = []
        for d in sorted(range(1, nt), key=lambda d: -min(d, nt - d)):
            out.append(remote(None, (lax.rem(t + d, nt), gx, gy), buffer.at[t], buffer.at[t]))
        for copy in out:
            copy.start()
        return out

    def put_bed_gradient(part, buffer):
        pack(buffer.at[t], (part.rows - 16) // 8, lambda r: part.bed_gradient(r, 8))
        return broadcast(buffer)

    odd = lax.rem(t, 2)
    pack(mine, ROWS // 8, lambda r: one.bed_gradient(r, 8))
    to_partner = remote(None, (t + 1 - 2 * odd, gx, gy), mine, theirs)
    to_partner.start()

    spots2 = [[[(1, 6), (0, 6)], [(1, 7), (0, 7)]], [[(2, 0), (1, 0)], [(2, 1), (1, 1)]]]
    from2 = [span(jnp.where(low, ROWS, MID), BLOCK), span(jnp.where(low, MID, 0), BLOCK)]
    arrive(early, True)
    for i in range(2):
        take(two, BLOCK * i, from2[i])
    two.coefficients()
    two.slopes()
    for k in range(STEPS):
        two.forward(k)
    fin_copies.append(send_final(two, fin_out2, fin2))
    arrive(late, True)
    beside(True)
    for i in range(2):
        demand(two, pull2, back2, foll2, BLOCK * i, from2[i], spots2[i])
    two.force()
    two.pull()
    sent2 = put_bed_gradient(two, sums2)
    to_partner.wait_recv()
    pair = t // 2
    pairs[pair] = mine[...] + theirs[...]
    exchanged = []
    for far in range(nt // 2 - 1, 0, -1):
        for parity in range(2):
            off = min((2 * far - parity) % nt, (2 * far + 1 - parity) % nt, key=lambda o: min(o, nt - o))
            copy = remote(odd == (parity + off) % 2, (lax.rem(t + nt - off, nt), gx, gy), pairs.at[pair], pairs.at[pair])
            exchanged.append((copy, odd == parity))
            when(odd == (parity + off) % 2, copy.start)
    lam_copies = [send_adjoint(one, lam_out1, lam1), send_adjoint(two, lam_out2, lam2)]

    for copy in fin_copies:
        when(before[0], copy.wait_recv)
    parts = ((one, pull1, back1, foll1, fin1, lam1, dest1), (two, pull2, back2, foll2, fin2, lam2, dest2))
    for part, pulls, back, foll, fin, lam, dest in parts:
        groups = (part.rows - 16) // 8
        for k in range(groups):
            rows, to = slice(8 + 8 * k, 16 + 8 * k), span(dest + 8 * k, 8)
            for p, came in enumerate(unpack(fin, groups, k)):
                begun = jnp.where(t == 0, back[p, rows], came)
                s0, s1 = part.field[p, S0, rows], part.field[p, S1, rows]
                field3[p, S0, to] = s0 - STATE_RATE * ((s0 - begun) + part.adj[p, 0, rows])
                field3[p, S1, to] = s1 - STATE_RATE * ((s1 - part.final[p, 0, rows]) + part.adj[p, 1, rows])
                field3[p, RATE, to] = part.field[p, RATE, rows]
                gain3[p, :, to] = part.gain[p, :, rows]
    again.coefficients()

    def to_rest(*fields):
        for p in range(2):
            for f in fields:
                field2[p, f, 0:END] = field3[p, f, MID - END:MID]

    to_rest(S0, S1, RATE)
    gain2[...] = gain3[:, :, MID - END:MID]
    rest.coefficients()

    def total(ref, rows):
        got = ref[0, rows]
        for i in range(1, ref.shape[0]):
            got = got + ref[i, rows]
        return got

    for copy, come in exchanged:
        when(come, copy.wait_recv)
    for copy in sent2:
        copy.wait_recv()
    for part, sums, dest in ((one, pairs, dest1), (two, sums2, dest2)):
        groups = (part.rows - 16) // 8
        sides = total(sums, slice(8 * groups, 8 * groups + 8))
        for k in range(groups):
            rows, to = slice(8 + 8 * k, 16 + 8 * k), span(dest + 8 * k, 8)
            main = total(sums, slice(8 * k, 8 * k + 8))
            side = jnp.where(within(at8, -8, 16), rolled(sides, -16 * k), 0.0)
            for p, got in enumerate((main, side)):
                field3[p, BED, to] = part.field[p, BED, rows] - BED_RATE * got
    to_rest(BED)

    again.slopes()
    for k in range(STEPS):
        again.forward(k)
    split = ROWS - EDGE
    fin_copies = [remote(*after, final3.at[0, 1, 8:8 + split], fin_last.at[0:split])]
    when(after[0], fin_copies[0].start)
    for copy in lam_copies:
        when(after[0], copy.wait_recv)
    for part, pulls, back, foll, fin, lam, dest in parts:
        groups = (part.rows - 16) // 8
        for k in range(groups):
            rows, to = slice(8 + 8 * k, 16 + 8 * k), span(dest + 8 * k, 8)
            for p, came in enumerate(unpack(lam, groups, k)):
                old = foll[p, rows]
                new = old - STATE_RATE * ((old - part.final[p, 1, rows]) + came)
                pull3[p, 0, to] = pulls[p, 0, rows] + field3[p, S1, to]
                pull3[p, 1, to] = pulls[p, 1, rows] + jnp.where(t < nt - 1, new, 0.0)

    for p in range(2):
        adj1[p, :, 0:ROWS] = pull3[p, :, 0:ROWS]
    again.force()
    again.pull()
    for r in range(0, split, BLOCK):
        sums3[t, r:r + BLOCK] = again.bed_gradient(8 + r, BLOCK)[0]
    sent3 = broadcast(sums3)

    for p in range(2):
        adj2[p, :, 0:END] = pull3[p, :, MID - END:MID]
    rest.slopes()
    for k in range(STEPS):
        rest.forward(k)
    fin_copies.append(remote(*after, final4.at[0, 1, 8:8 + EDGE], fin_last.at[split:ROWS]))
    when(after[0], fin_copies[1].start)
    rest.force()
    rest.pull()
    sums4[t] = rest.bed_gradient(8, EDGE)[0]
    sent4 = broadcast(sums4)

    for copy in fin_copies:
        when(before[0], copy.wait_recv)
    for r in range(0, ROWS, BLOCK):
        rows, short = slice(8 + r, 8 + r + BLOCK), slice(r, r + BLOCK)
        part, own = (again, rows) if r < split else (rest, slice(8, 8 + EDGE))
        begun = jnp.where(t == 0, ff[BACK, span(home + r, BLOCK)], fin_last[short])
        s0, s1 = field3[0, S0, rows], field3[0, S1, rows]
        states_out[0, short] = s0 - STATE_RATE * ((s0 - begun) + part.adj[0, 0, own])
        states_out[1, short] = s1 - STATE_RATE * ((s1 - part.final[0, 0, own]) + part.adj[0, 1, own])
    for copy in sent3 + sent4:
        copy.wait_recv()
    for r in range(0, ROWS, BLOCK):
        rows, short = slice(8 + r, 8 + r + BLOCK), slice(r, r + BLOCK)
        now = field3[0, BED, rows]
        sums = total(sums3, short) if r < split else total(sums4, slice(0, EDGE))
        bed_out[short] = now - BED_RATE * (sums + (now - ff[BED, span(home + r, BLOCK)]))
    for copy, to in copies:
        when(to, copy.wait_send)


def emit(states, bed, states_out, bed_out, sem):
    copies = [pltpu.make_async_copy(src, dst, sem.at[i]) for i, (src, dst) in enumerate(((states, states_out), (bed, bed_out)))]
    for copy in copies:
        copy.start()
    for copy in copies:
        copy.wait()


def solution(mesh):
    nt, nx, ny = (mesh.shape[a] for a in ("tm", "gx", "gy"))
    f32 = jnp.float32

    def vmem(*shape, dtype=f32):
        return pltpu.VMEM(shape, dtype)

    def model_scratch(rows):
        return [
            vmem(2, 4, rows + 8, COLS), vmem(2, 2, rows, COLS), vmem(2, 2, rows, COLS),
            vmem(STEPS - 1, 2, 2, rows + 8, COLS), vmem(2, 2, rows + 8, COLS), vmem(2, 2, 8 + rows, COLS),
            vmem(2, 2, 8 + rows, COLS), vmem(2, 2, rows, COLS), vmem(2, 2, rows, COLS),
        ]

    def step(states, bed, background, mask, rate, cells, values):
        obs = cells.shape[-1]
        count = 23 + 6 + 2 + 2 + 2 + 1 + 2 * (nt // 2 - 1) + 3 * (nt - 1)
        out = pl.pallas_call(
            functools.partial(kernel, nt, nx, ny),
            out_shape=(pltpu.VMEM(states.shape, f32), pltpu.VMEM(bed.shape, f32)),
            out_specs=(pl.BlockSpec(memory_space=pltpu.VMEM),) * 2,
            in_specs=[pl.BlockSpec(memory_space=pltpu.HBM)] * 7,
            scratch_shapes=[
                vmem(FIELDS, HIGH, COLS),
                vmem(ROWS, COLS), vmem(ROWS, COLS, dtype=jnp.int32),
                vmem(2, 1, 1, obs, dtype=jnp.int32), vmem(2, 1, 1, obs),
                vmem(2, 2, 1, 1, obs, dtype=jnp.int32), vmem(2, 2, 1, 1, obs),
                vmem(ROWS, COLS), vmem(ROWS, COLS), vmem(HIGH, COLS), vmem(HIGH, COLS),
                vmem(HIGH, COLS), vmem(2, 2, 8, COLS), vmem(2, 3, 8, COLS), vmem(2, MID, COLS), vmem(2, END, COLS),
                *model_scratch(MID), *model_scratch(END),
                vmem(2, 4, MID + 8, COLS), vmem(2, 2, MID, COLS), vmem(2, 2, ROWS, COLS), vmem(2, 2, END, COLS),
                vmem(2, 2, MID, COLS), vmem(2, 2, END, COLS), vmem(2, 2, MID, COLS),
                vmem(2, MID, COLS), vmem(2, END, COLS),
                vmem(ROWS + 8, COLS), vmem(ROWS + 8, COLS), vmem(nt // 2, ROWS + 8, COLS), vmem(nt, EDGE + 8, COLS),
                vmem(nt, ROWS - EDGE, COLS), vmem(nt, EDGE, COLS),
                vmem(ROWS + 8, COLS), vmem(EDGE + 8, COLS), vmem(ROWS + 8, COLS), vmem(EDGE + 8, COLS), vmem(ROWS, COLS),
                vmem(ROWS + 8, COLS), vmem(EDGE + 8, COLS), vmem(ROWS + 8, COLS), vmem(EDGE + 8, COLS),
                pltpu.SemaphoreType.DMA((7,)),
                pltpu.SemaphoreType.DMA((count,)), pltpu.SemaphoreType.DMA((count,)),
            ],
            compiler_params=pltpu.CompilerParams(
                collective_id=0, has_side_effects=True, vmem_limit_bytes=32 << 20),
            name="assimilate",
        )(*(pltpu.with_memory_space_constraint(x, pltpu.HBM)
            for x in (states, bed, background, mask, rate, cells, values)))
        return pl.pallas_call(
            emit,
            out_shape=(jax.ShapeDtypeStruct(states.shape, f32), jax.ShapeDtypeStruct(bed.shape, f32)),
            in_specs=[pl.BlockSpec(memory_space=pltpu.VMEM)] * 2,
            out_specs=(pl.BlockSpec(memory_space=pl.ANY),) * 2,
            scratch_shapes=[pltpu.SemaphoreType.DMA((2,))],
            compiler_params=pltpu.CompilerParams(vmem_limit_bytes=1 << 20),
            name="emit",
        )(*(pltpu.with_memory_space_constraint(x, pltpu.VMEM) for x in out))

    return jax.shard_map(
        step,
        mesh=mesh,
        in_specs=(P("tm", "gx", "gy"),) + (P("gx", "gy"),) * 4 + (P("tm", "gx", "gy", None),) * 2,
        out_specs=(P("tm", "gx", "gy"), P("gx", "gy")),
        check_vma=False,
    )
```

time: 218 us -> 43.7 us (0.20)
  the two profiles are of different devices: /device:TPU:56 before, /device:TPU:6 now
where the time goes in v2:
time: 43.7 us; the launch traced here: 43.6 us
  Pallas kernels  42.9 us (98%)
  between operations  0.64 us (1%)
    pallas_call x1, Pallas kernels, step(): pl.pallas_call(functools.partial(kernel, nt, nx, ny), out_shape=(pltpu.VM...  42.3 us

profile of v2, /device:TPU:6, one launch (start us, length us, event | category | flops | bytes accessed | tf_op | source)
XLA Modules:
  0.0 43.6 jit_solution(1064900259094015811)
XLA Ops:
  0.6 42.3 %assimilate.1 = (f32[2,64,128]{2,1,0:T(8,128)S(1)}, f32[64,128]{1,0:T(8,128)S(1)}) custom-call(f32[2,64,128]{2,1,0:T(8,128)} %states.1, f32[64,128]{1,0:T(8,128)} %bed.1, f32[64,128]{1,0:T(8,128)} %background.1, s32[64,128]{1,0:T(8,128)} %mask.1, f32[64,128]{1,0:T(8,128)} %rate.1, s32[2,1,1,512]{3,2,1,0:T(1,128)} %cells.1, f32[2,1,1,512]{3,2,1,0:T(1,128)} %values.1), custom_call_target="tpu_custom_call" | custom-call | tf_op jit(solution)/shard_map/assimilate/pallas_call | solution.py:616
  42.9 0.7 %emit.1 = (f32[2,64,128]{2,1,0:T(8,128)}, f32[64,128]{1,0:T(8,128)}) custom-call(f32[2,64,128]{2,1,0:T(8,128)S(1)} %get-tuple-element.4.states, f32[64,128]{1,0:T(8,128)S(1)} %get-tuple-element.5.bed), custom_call_target="tpu_custom_call" | custom-call | tf_op jit(solution)/shard_map/emit/pallas_call | solution.py:644

commit v3 on v2

--- a/solution.py
+++ b/solution.py
@@ -179,9 +179,9 @@
     nxt, fold_out, fold_in, foll1, foll2,
     field1, coef1, slope1, path1, adj1, flux1, grad1, gain1, final1,
     field2, coef2, slope2, path2, adj2, flux2, grad2, gain2, final2,
-    field3, gain3, final3, final4,
-    pull1, pull2, pull3, back1, back2,
-    mine, theirs, pairs, sums2, sums3, sums4, fin_out1, fin_out2, fin1, fin2, fin_last, lam_out1, lam_out2, lam1, lam2,
+    field3, gain3, final3, field4, gain4, final4,
+    pull1, pull2, pull3, pull4, back1, back2,
+    mine, theirs, pairs, sums2, sums3, sums4, fin_out1, fin_out2, fin1, fin2, fin3, fin4, lam_out1, lam_out2, lam1, lam2,
     load_sem, send_sem, recv_sem,
 ):
     t, gx, gy = lax.axis_index("tm"), lax.axis_index("gx"), lax.axis_index("gy")
@@ -249,8 +249,8 @@
     one = Model(MID, field1, coef1, slope1, path1, adj1, flux1, grad1, gain1, final1)
     two = Model(END, field2, coef2, slope2, path2, adj2, flux2, grad2, gain2, final2)
     again = Model(ROWS, field3, coef1, slope1, path1, adj1, flux1, grad1, gain3, final3)
-    rest = Model(END, field2, coef2, slope2, path2, adj2, flux2, grad2, gain2, final4)
-    for part in (one, two):
+    rest = Model(END, field4, coef2, slope2, path2, adj2, flux2, grad2, gain4, final4)
+    for part in (one, two, again, rest):
         part.clear_ends()
 
     loads[0].wait()
@@ -341,7 +341,6 @@
 
     for copy, to, _, _ in onward:
         when(to, copy.start)
-    late += onward
 
     def arrive(group, far):
         for copy, _, come, dx in group:
@@ -435,7 +434,6 @@
         demand(one, pull1, back1, foll1, r, slice(r, r + BLOCK), spots)
     one.force()
 
-    dest1, dest2 = jnp.where(low, 0, EDGE), jnp.where(low, ROWS, 0)
     one.pull()
 
     def broadcast(buffer):
@@ -467,6 +465,7 @@
     fin_copies.append(send_final(two, fin_out2, fin2))
     arrive(late, True)
     beside(True)
+    arrive(onward, True)
     for i in range(2):
         demand(two, pull2, back2, foll2, BLOCK * i, from2[i], spots2[i])
     two.force()
@@ -484,29 +483,44 @@
             when(odd == (parity + off) % 2, copy.start)
     lam_copies = [send_adjoint(one, lam_out1, lam1), send_adjoint(two, lam_out2, lam2)]
 
-    for copy in fin_copies:
-        when(before[0], copy.wait_recv)
-    parts = ((one, pull1, back1, foll1, fin1, lam1, dest1), (two, pull2, back2, foll2, fin2, lam2, dest2))
-    for part, pulls, back, foll, fin, lam, dest in parts:
+    def renew(part, pulls, back, foll, fin, lam, field, gain, pull, start):
         groups = (part.rows - 16) // 8
         for k in range(groups):
-            rows, to = slice(8 + 8 * k, 16 + 8 * k), span(dest + 8 * k, 8)
-            for p, came in enumerate(unpack(fin, groups, k)):
-                begun = jnp.where(t == 0, back[p, rows], came)
+            rows, to = slice(8 + 8 * k, 16 + 8 * k), span(start + 8 * k, 8)
+            came, came_lam = unpack(fin, groups, k), unpack(lam, groups, k)
+            for p in range(2):
+                begun = jnp.where(t == 0, back[p, rows], came[p])
                 s0, s1 = part.field[p, S0, rows], part.field[p, S1, rows]
-                field3[p, S0, to] = s0 - STATE_RATE * ((s0 - begun) + part.adj[p, 0, rows])
-                field3[p, S1, to] = s1 - STATE_RATE * ((s1 - part.final[p, 0, rows]) + part.adj[p, 1, rows])
-                field3[p, RATE, to] = part.field[p, RATE, rows]
-                gain3[p, :, to] = part.gain[p, :, rows]
-    again.coefficients()
+                field[p, S0, to] = s0 - STATE_RATE * ((s0 - begun) + part.adj[p, 0, rows])
+                new1 = s1 - STATE_RATE * ((s1 - part.final[p, 0, rows]) + part.adj[p, 1, rows])
+                field[p, S1, to] = new1
+                field[p, RATE, to] = part.field[p, RATE, rows]
+                gain[p, :, to] = part.gain[p, :, rows]
+                old = foll[p, rows]
+                new = old - STATE_RATE * ((old - part.final[p, 1, rows]) + came_lam[p])
+                pull[p, 0, to] = pulls[p, 0, rows] + new1
+                pull[p, 1, to] = pulls[p, 1, rows] + jnp.where(t < nt - 1, new, 0.0)
+
+    far_at, beside_at, beside_from = jnp.where(low, EDGE, 0), jnp.where(low, 0, EDGE), jnp.where(low, ROWS - EDGE, 0)
 
     def to_rest(*fields):
         for p in range(2):
             for f in fields:
-                field2[p, f, 0:END] = field3[p, f, MID - END:MID]
-
+                field4[p, f, span(beside_at, EDGE)] = field3[p, f, span(beside_from, EDGE)]
+
+    when(before[0], fin_copies[0].wait_recv)
+    when(after[0], lam_copies[0].wait_recv)
+    renew(one, pull1, back1, foll1, fin1, lam1, field3, gain3, pull3, 0)
+    again.coefficients()
+    when(before[0], fin_copies[1].wait_recv)
+    when(after[0], lam_copies[1].wait_recv)
+    renew(two, pull2, back2, foll2, fin2, lam2, field4, gain4, pull4, far_at)
     to_rest(S0, S1, RATE)
-    gain2[...] = gain3[:, :, MID - END:MID]
+    for p in range(2):
+        gain4[p, :, span(beside_at, EDGE)] = gain3[p, :, span(beside_from, EDGE)]
+        pull4[p, :, span(beside_at, EDGE)] = pull3[p, :, span(beside_from, EDGE)]
+        adj1[p, :, 0:ROWS] = pull3[p]
+        adj2[p, :, 0:END] = pull4[p]
     rest.coefficients()
 
     def total(ref, rows):
@@ -515,75 +529,58 @@
             got = got + ref[i, rows]
         return got
 
-    for copy, come in exchanged:
-        when(come, copy.wait_recv)
-    for copy in sent2:
-        copy.wait_recv()
-    for part, sums, dest in ((one, pairs, dest1), (two, sums2, dest2)):
+    def new_bed(part, sums, field, start):
         groups = (part.rows - 16) // 8
         sides = total(sums, slice(8 * groups, 8 * groups + 8))
         for k in range(groups):
-            rows, to = slice(8 + 8 * k, 16 + 8 * k), span(dest + 8 * k, 8)
+            rows, to = slice(8 + 8 * k, 16 + 8 * k), span(start + 8 * k, 8)
             main = total(sums, slice(8 * k, 8 * k + 8))
             side = jnp.where(within(at8, -8, 16), rolled(sides, -16 * k), 0.0)
             for p, got in enumerate((main, side)):
-                field3[p, BED, to] = part.field[p, BED, rows] - BED_RATE * got
+                field[p, BED, to] = part.field[p, BED, rows] - BED_RATE * got
+
+    for copy, come in exchanged:
+        when(come, copy.wait_recv)
+    new_bed(one, pairs, field3, 0)
+
+    split = ROWS - EDGE
+
+    def descend(part, into, sums, count):
+        part.slopes()
+        for k in range(STEPS):
+            part.forward(k)
+        copy = remote(*after, part.final.at[0, 1, 8:8 + count], into)
+        when(after[0], copy.start)
+        part.force()
+        part.pull()
+        for r in range(0, count, BLOCK):
+            sums[t, r:r + BLOCK] = part.bed_gradient(8 + r, BLOCK)[0]
+        return copy, broadcast(sums)
+
+    fin3_copy, sent3 = descend(again, fin3, sums3, split)
+    for copy in sent2:
+        copy.wait_recv()
+    new_bed(two, sums2, field4, far_at)
     to_rest(BED)
-
-    again.slopes()
-    for k in range(STEPS):
-        again.forward(k)
-    split = ROWS - EDGE
-    fin_copies = [remote(*after, final3.at[0, 1, 8:8 + split], fin_last.at[0:split])]
-    when(after[0], fin_copies[0].start)
-    for copy in lam_copies:
-        when(after[0], copy.wait_recv)
-    for part, pulls, back, foll, fin, lam, dest in parts:
-        groups = (part.rows - 16) // 8
-        for k in range(groups):
-            rows, to = slice(8 + 8 * k, 16 + 8 * k), span(dest + 8 * k, 8)
-            for p, came in enumerate(unpack(lam, groups, k)):
-                old = foll[p, rows]
-                new = old - STATE_RATE * ((old - part.final[p, 1, rows]) + came)
-                pull3[p, 0, to] = pulls[p, 0, rows] + field3[p, S1, to]
-                pull3[p, 1, to] = pulls[p, 1, rows] + jnp.where(t < nt - 1, new, 0.0)
-
-    for p in range(2):
-        adj1[p, :, 0:ROWS] = pull3[p, :, 0:ROWS]
-    again.force()
-    again.pull()
-    for r in range(0, split, BLOCK):
-        sums3[t, r:r + BLOCK] = again.bed_gradient(8 + r, BLOCK)[0]
-    sent3 = broadcast(sums3)
-
-    for p in range(2):
-        adj2[p, :, 0:END] = pull3[p, :, MID - END:MID]
-    rest.slopes()
-    for k in range(STEPS):
-        rest.forward(k)
-    fin_copies.append(remote(*after, final4.at[0, 1, 8:8 + EDGE], fin_last.at[split:ROWS]))
-    when(after[0], fin_copies[1].start)
-    rest.force()
-    rest.pull()
-    sums4[t] = rest.bed_gradient(8, EDGE)[0]
-    sent4 = broadcast(sums4)
-
-    for copy in fin_copies:
+    fin4_copy, sent4 = descend(rest, fin4, sums4, EDGE)
+
+    out3, out4 = jnp.where(low, 0, EDGE), jnp.where(low, split, 0)
+    both_passes = ((again, fin3, fin3_copy, sent3, sums3, split, out3), (rest, fin4, fin4_copy, sent4, sums4, EDGE, out4))
+    for part, fin, copy, _, _, count, out in both_passes:
         when(before[0], copy.wait_recv)
-    for r in range(0, ROWS, BLOCK):
-        rows, short = slice(8 + r, 8 + r + BLOCK), slice(r, r + BLOCK)
-        part, own = (again, rows) if r < split else (rest, slice(8, 8 + EDGE))
-        begun = jnp.where(t == 0, ff[BACK, span(home + r, BLOCK)], fin_last[short])
-        s0, s1 = field3[0, S0, rows], field3[0, S1, rows]
-        states_out[0, short] = s0 - STATE_RATE * ((s0 - begun) + part.adj[0, 0, own])
-        states_out[1, short] = s1 - STATE_RATE * ((s1 - part.final[0, 0, own]) + part.adj[0, 1, own])
-    for copy in sent3 + sent4:
-        copy.wait_recv()
-    for r in range(0, ROWS, BLOCK):
-        rows, short = slice(8 + r, 8 + r + BLOCK), slice(r, r + BLOCK)
-        now = field3[0, BED, rows]
-        sums = total(sums3, short) if r < split else total(sums4, slice(0, EDGE))
-        bed_out[short] = now - BED_RATE * (sums + (now - ff[BED, span(home + r, BLOCK)]))
+        for r in range(0, count, BLOCK):
+            rows, short, to = slice(8 + r, 8 + r + BLOCK), slice(r, r + BLOCK), span(out + r, BLOCK)
+            begun = jnp.where(t == 0, ff[BACK, span(home + out + r, BLOCK)], fin[short])
+            s0, s1 = part.field[0, S0, rows], part.field[0, S1, rows]
+            states_out[0, to] = s0 - STATE_RATE * ((s0 - begun) + part.adj[0, 0, rows])
+            states_out[1, to] = s1 - STATE_RATE * ((s1 - part.final[0, 0, rows]) + part.adj[0, 1, rows])
+    for part, _, _, sent, sums, count, out in both_passes:
+        for copy in sent:
+            copy.wait_recv()
+        for r in range(0, count, BLOCK):
+            rows, short, to = slice(8 + r, 8 + r + BLOCK), slice(r, r + BLOCK), span(out + r, BLOCK)
+            now = part.field[0, BED, rows]
+            bed_out[to] = now - BED_RATE * (total(sums, short) + (now - ff[BED, span(home + out + r, BLOCK)]))
     for copy, to in copies:
         when(to, copy.wait_send)
 
@@ -626,12 +623,14 @@
                 vmem(ROWS, COLS), vmem(ROWS, COLS), vmem(HIGH, COLS), vmem(HIGH, COLS),
                 vmem(HIGH, COLS), vmem(2, 2, 8, COLS), vmem(2, 3, 8, COLS), vmem(2, MID, COLS), vmem(2, END, COLS),
                 *model_scratch(MID), *model_scratch(END),
-                vmem(2, 4, MID + 8, COLS), vmem(2, 2, MID, COLS), vmem(2, 2, ROWS, COLS), vmem(2, 2, END, COLS),
-                vmem(2, 2, MID, COLS), vmem(2, 2, END, COLS), vmem(2, 2, MID, COLS),
+                vmem(2, 4, ROWS + 8, COLS), vmem(2, 2, ROWS, COLS), vmem(2, 2, ROWS, COLS),
+                vmem(2, 4, END + 8, COLS), vmem(2, 2, END, COLS), vmem(2, 2, END, COLS),
+                vmem(2, 2, MID, COLS), vmem(2, 2, END, COLS), vmem(2, 2, ROWS, COLS), vmem(2, 2, END, COLS),
                 vmem(2, MID, COLS), vmem(2, END, COLS),
                 vmem(ROWS + 8, COLS), vmem(ROWS + 8, COLS), vmem(nt // 2, ROWS + 8, COLS), vmem(nt, EDGE + 8, COLS),
                 vmem(nt, ROWS - EDGE, COLS), vmem(nt, EDGE, COLS),
-                vmem(ROWS + 8, COLS), vmem(EDGE + 8, COLS), vmem(ROWS + 8, COLS), vmem(EDGE + 8, COLS), vmem(ROWS, COLS),
+                vmem(ROWS + 8, COLS), vmem(EDGE + 8, COLS), vmem(ROWS + 8, COLS), vmem(EDGE + 8, COLS),
+                vmem(ROWS - EDGE, COLS), vmem(EDGE, COLS),
                 vmem(ROWS + 8, COLS), vmem(EDGE + 8, COLS), vmem(ROWS + 8, COLS), vmem(EDGE + 8, COLS),
                 pltpu.SemaphoreType.DMA((7,)),
                 pltpu.SemaphoreType.DMA((count,)), pltpu.SemaphoreType.DMA((count,)),

time: 43.7 us -> 43.5 us (level)
  no operation moved by 1% of the time
where the time goes in v3:
time: 43.5 us; the launch traced here: 43.4 us
  Pallas kernels  42.7 us (98%)
  between operations  0.64 us (1%)
    pallas_call x1, Pallas kernels, step(): pl.pallas_call(functools.partial(kernel, nt, nx, ny), out_shape=(pltpu.VM...  42.1 us

profile of v3, /device:TPU:6, one launch (start us, length us, event | category | flops | bytes accessed | tf_op | source)
XLA Modules:
  0.0 43.4 jit_solution(9426591640550521322)
XLA Ops:
  0.6 42.1 %assimilate.1 = (f32[2,64,128]{2,1,0:T(8,128)S(1)}, f32[64,128]{1,0:T(8,128)S(1)}) custom-call(f32[2,64,128]{2,1,0:T(8,128)} %states.1, f32[64,128]{1,0:T(8,128)} %bed.1, f32[64,128]{1,0:T(8,128)} %background.1, s32[64,128]{1,0:T(8,128)} %mask.1, f32[64,128]{1,0:T(8,128)} %rate.1, s32[2,1,1,512]{3,2,1,0:T(1,128)} %cells.1, f32[2,1,1,512]{3,2,1,0:T(1,128)} %values.1), custom_call_target="tpu_custom_call" | custom-call | tf_op jit(solution)/shard_map/assimilate/pallas_call | solution.py:613
  42.7 0.7 %emit.1 = (f32[2,64,128]{2,1,0:T(8,128)}, f32[64,128]{1,0:T(8,128)}) custom-call(f32[2,64,128]{2,1,0:T(8,128)S(1)} %get-tuple-element.4.states, f32[64,128]{1,0:T(8,128)S(1)} %get-tuple-element.5.bed), custom_call_target="tpu_custom_call" | custom-call | tf_op jit(solution)/shard_map/emit/pallas_call | solution.py:643

commit v4 on v3

--- a/solution.py
+++ b/solution.py
@@ -81,8 +81,8 @@
 
 
 class Model:
-    def __init__(self, rows, field, coef, slope, path, adj, flux, grad, gain, final):
-        self.rows, self.field, self.coef, self.slope, self.path = rows, field, coef, slope, path
+    def __init__(self, rows, field, coef, slope, path, kept, adj, flux, grad, gain, final):
+        self.rows, self.field, self.coef, self.slope, self.path, self.kept = rows, field, coef, slope, path, kept
         self.adj, self.flux, self.grad, self.gain, self.final = adj, flux, grad, gain, final
 
     def blocks(self):
@@ -115,16 +115,20 @@
     def thick(self, k, p, rows):
         return self.field[p, S0:S1 + 1, rows] if k == 0 else self.path[k - 1, p, :, rows]
 
-    def faces(self, k, rows):
-        here = [self.thick(k, p, rows) for p in range(2)]
-        up = [[self.thick(k, p, slice(rows.start + 1, rows.stop + 1)) for p in range(2)], ahead(*here)]
-        mean = [[0.5 * (here[p] + up[d][p]) for p in range(2)] for d in range(2)]
-        step = [[(up[d][p] - here[p]) + self.slope[d, p, rows] for p in range(2)] for d in range(2)]
-        return here, mean, step
+    def down(self, k, rows, here):
+        up = [self.thick(k, p, slice(rows.start + 1, rows.stop + 1)) for p in range(2)]
+        return [0.5 * (here[p] + up[p]) for p in range(2)], [(up[p] - here[p]) + self.slope[0, p, rows] for p in range(2)]
+
+    def across(self, rows, here):
+        up = ahead(*here)
+        return [0.5 * (here[p] + up[p]) for p in range(2)], [(up[p] - here[p]) + self.slope[1, p, rows] for p in range(2)]
 
     def forward(self, k):
         for rows in self.blocks():
-            here, mean, step = self.faces(k, rows)
+            here = [self.thick(k, p, rows) for p in range(2)]
+            mean, step = zip(self.down(k, rows, here), self.across(rows, here))
+            for p in range(2):
+                self.kept[k, 0, p, :, rows], self.kept[k, 1, p, :, rows] = mean[1][p], step[1][p]
             f = [[self.coef[d, p, rows] * mean[d][p] * mean[d][p] * step[d][p] for p in range(2)] for d in range(2)]
             left = behind(*f[1])
             for p in range(2):
@@ -142,7 +146,8 @@
 
     def backward(self, k):
         for rows in self.blocks():
-            _, mean, step = self.faces(k, rows)
+            down = self.down(k, rows, [self.thick(k, p, rows) for p in range(2)])
+            mean, step = ([down[i], [self.kept[k, i, p, :, rows] for p in range(2)]] for i in range(2))
             lam = [self.adj[p, :, rows] for p in range(2)]
             up = [[self.adj[p, :, rows.start + 1:rows.stop + 1] for p in range(2)], ahead(*lam)]
             spot = slice(8 + rows.start, 8 + rows.stop)
@@ -177,8 +182,8 @@
     states_out, bed_out,
     ff, rate_in, mask_in, cell_in, value_in, cell_near, value_near, left_out, right_out, left_in, right_in,
     nxt, fold_out, fold_in, foll1, foll2,
-    field1, coef1, slope1, path1, adj1, flux1, grad1, gain1, final1,
-    field2, coef2, slope2, path2, adj2, flux2, grad2, gain2, final2,
+    field1, coef1, slope1, path1, kept1, adj1, flux1, grad1, gain1, final1,
+    field2, coef2, slope2, path2, kept2, adj2, flux2, grad2, gain2, final2,
     field3, gain3, final3, field4, gain4, final4,
     pull1, pull2, pull3, pull4, back1, back2,
     mine, theirs, pairs, sums2, sums3, sums4, fin_out1, fin_out2, fin1, fin2, fin3, fin4, lam_out1, lam_out2, lam1, lam2,
@@ -246,10 +251,10 @@
     clear(gy == ny - 1, (right_in, ...), (fold_in, 1))
     clear(t == nt - 1, (nxt, ...), (fold_in, ...))
 
-    one = Model(MID, field1, coef1, slope1, path1, adj1, flux1, grad1, gain1, final1)
-    two = Model(END, field2, coef2, slope2, path2, adj2, flux2, grad2, gain2, final2)
-    again = Model(ROWS, field3, coef1, slope1, path1, adj1, flux1, grad1, gain3, final3)
-    rest = Model(END, field4, coef2, slope2, path2, adj2, flux2, grad2, gain4, final4)
+    one = Model(MID, field1, coef1, slope1, path1, kept1, adj1, flux1, grad1, gain1, final1)
+    two = Model(END, field2, coef2, slope2, path2, kept2, adj2, flux2, grad2, gain2, final2)
+    again = Model(ROWS, field3, coef1, slope1, path1, kept1, adj1, flux1, grad1, gain3, final3)
+    rest = Model(END, field4, coef2, slope2, path2, kept2, adj2, flux2, grad2, gain4, final4)
     for part in (one, two, again, rest):
         part.clear_ends()
 
@@ -436,12 +441,22 @@
 
     one.pull()
 
-    def broadcast(buffer):
-        out = []
-        for d in sorted(range(1, nt), key=lambda d: -min(d, nt - d)):
+    def broadcast(buffer, in_order=False):
+        out, base = [], len(copies)
+        for d in sorted(range(1, nt), key=lambda d: d if in_order else -min(d, nt - d)):
             out.append(remote(None, (lax.rem(t + d, nt), gx, gy), buffer.at[t], buffer.at[t]))
-        for copy in out:
-            copy.start()
+        if not in_order:
+            for copy in out:
+                copy.start()
+            return out
+        for i in range(nt):
+            spot = lax.rem(i + nt - t, nt) + base - 1
+
+            @pl.when(t != i)
+            def _():
+                pltpu.make_async_remote_copy(
+                    src_ref=buffer.at[t], dst_ref=buffer.at[t], send_sem=send_sem.at[spot], recv_sem=recv_sem.at[spot],
+                    device_id=(i, gx, gy), device_id_type=MESH).start()
         return out
 
     def put_bed_gradient(part, buffer):
@@ -469,8 +484,8 @@
     for i in range(2):
         demand(two, pull2, back2, foll2, BLOCK * i, from2[i], spots2[i])
     two.force()
-    two.pull()
-    sent2 = put_bed_gradient(two, sums2)
+    for k in (3, 2):
+        two.backward(k)
     to_partner.wait_recv()
     pair = t // 2
     pairs[pair] = mine[...] + theirs[...]
@@ -481,6 +496,9 @@
             copy = remote(odd == (parity + off) % 2, (lax.rem(t + nt - off, nt), gx, gy), pairs.at[pair], pairs.at[pair])
             exchanged.append((copy, odd == parity))
             when(odd == (parity + off) % 2, copy.start)
+    for k in (1, 0):
+        two.backward(k)
+    sent2 = put_bed_gradient(two, sums2)
     lam_copies = [send_adjoint(one, lam_out1, lam1), send_adjoint(two, lam_out2, lam2)]
 
     def renew(part, pulls, back, foll, fin, lam, field, gain, pull, start):
@@ -555,7 +573,7 @@
         part.pull()
         for r in range(0, count, BLOCK):
             sums[t, r:r + BLOCK] = part.bed_gradient(8 + r, BLOCK)[0]
-        return copy, broadcast(sums)
+        return copy, broadcast(sums, True)
 
     fin3_copy, sent3 = descend(again, fin3, sums3, split)
     for copy in sent2:
@@ -603,7 +621,8 @@
     def model_scratch(rows):
         return [
             vmem(2, 4, rows + 8, COLS), vmem(2, 2, rows, COLS), vmem(2, 2, rows, COLS),
-            vmem(STEPS - 1, 2, 2, rows + 8, COLS), vmem(2, 2, rows + 8, COLS), vmem(2, 2, 8 + rows, COLS),
+            vmem(STEPS - 1, 2, 2, rows + 8, COLS), vmem(STEPS, 2, 2, 2, rows, COLS),
+            vmem(2, 2, rows + 8, COLS), vmem(2, 2, 8 + rows, COLS),
             vmem(2, 2, 8 + rows, COLS), vmem(2, 2, rows, COLS), vmem(2, 2, rows, COLS),
         ]
 

time: 43.5 us -> 42.2 us (0.970)
  Pallas kernels: 42.7 us -> 41.3 us
    pallas_call x1, Pallas kernels: 42.1 us -> 40.6 us  [step(): pl.pallas_call(functools.partial(kernel, nt, nx, ny), out_shape=(pltpu.VM...]
where the time goes in v4:
time: 42.2 us; the launch traced here: 41.9 us
  Pallas kernels  41.3 us (98%)
  between operations  0.64 us (2%)
    pallas_call x1, Pallas kernels, step(): pl.pallas_call(functools.partial(kernel, nt, nx, ny), out_shape=(pltpu.VM...  40.6 us

profile of v4, /device:TPU:6, one launch (start us, length us, event | category | flops | bytes accessed | tf_op | source)
XLA Modules:
  0.0 41.9 jit_solution(5972028870973998160)
XLA Ops:
  0.6 40.6 %assimilate.1 = (f32[2,64,128]{2,1,0:T(8,128)S(1)}, f32[64,128]{1,0:T(8,128)S(1)}) custom-call(f32[2,64,128]{2,1,0:T(8,128)} %states.1, f32[64,128]{1,0:T(8,128)} %bed.1, f32[64,128]{1,0:T(8,128)} %background.1, s32[64,128]{1,0:T(8,128)} %mask.1, f32[64,128]{1,0:T(8,128)} %rate.1, s32[2,1,1,512]{3,2,1,0:T(1,128)} %cells.1, f32[2,1,1,512]{3,2,1,0:T(1,128)} %values.1), custom_call_target="tpu_custom_call" | custom-call | tf_op jit(solution)/shard_map/assimilate/pallas_call | solution.py:632
  41.3 0.7 %emit.1 = (f32[2,64,128]{2,1,0:T(8,128)}, f32[64,128]{1,0:T(8,128)}) custom-call(f32[2,64,128]{2,1,0:T(8,128)S(1)} %get-tuple-element.4.states, f32[64,128]{1,0:T(8,128)S(1)} %get-tuple-element.5.bed), custom_call_target="tpu_custom_call" | custom-call | tf_op jit(solution)/shard_map/emit/pallas_call | solution.py:662

commit v5 on v4

--- a/solution.py
+++ b/solution.py
@@ -449,15 +449,18 @@
             for copy in out:
                 copy.start()
             return out
-        for i in range(nt):
-            spot = lax.rem(i + nt - t, nt) + base - 1
-
-            @pl.when(t != i)
-            def _():
-                pltpu.make_async_remote_copy(
-                    src_ref=buffer.at[t], dst_ref=buffer.at[t], send_sem=send_sem.at[spot], recv_sem=recv_sem.at[spot],
-                    device_id=(i, gx, gy), device_id_type=MESH).start()
-        return out
+        def begin(targets):
+            for i in targets:
+                spot = lax.rem(i + nt - t, nt) + base - 1
+
+                @pl.when(t != i)
+                def _():
+                    pltpu.make_async_remote_copy(
+                        src_ref=buffer.at[t], dst_ref=buffer.at[t], send_sem=send_sem.at[spot], recv_sem=recv_sem.at[spot],
+                        device_id=(i, gx, gy), device_id_type=MESH).start()
+
+        begin(range(nt // 2))
+        return out, functools.partial(begin, range(nt // 2, nt))
 
     def put_bed_gradient(part, buffer):
         pack(buffer.at[t], (part.rows - 16) // 8, lambda r: part.bed_gradient(r, 8))
@@ -575,12 +578,14 @@
             sums[t, r:r + BLOCK] = part.bed_gradient(8 + r, BLOCK)[0]
         return copy, broadcast(sums, True)
 
-    fin3_copy, sent3 = descend(again, fin3, sums3, split)
+    fin3_copy, (sent3, begin3) = descend(again, fin3, sums3, split)
     for copy in sent2:
         copy.wait_recv()
     new_bed(two, sums2, field4, far_at)
     to_rest(BED)
-    fin4_copy, sent4 = descend(rest, fin4, sums4, EDGE)
+    fin4_copy, (sent4, begin4) = descend(rest, fin4, sums4, EDGE)
+    begin3()
+    begin4()
 
     out3, out4 = jnp.where(low, 0, EDGE), jnp.where(low, split, 0)
     both_passes = ((again, fin3, fin3_copy, sent3, sums3, split, out3), (rest, fin4, fin4_copy, sent4, sums4, EDGE, out4))

time: 42.2 us -> 41.6 us (0.986)
  Pallas kernels: 41.3 us -> 40.8 us
    pallas_call x1, Pallas kernels: 40.6 us -> 40.2 us  [step(): pl.pallas_call(functools.partial(kernel, nt, nx, ny), out_shape=(pltpu.VM...]
where the time goes in v5:
time: 41.6 us; the launch traced here: 41.5 us
  Pallas kernels  40.8 us (98%)
  between operations  0.64 us (2%)
    pallas_call x1, Pallas kernels, step(): pl.pallas_call(functools.partial(kernel, nt, nx, ny), out_shape=(pltpu.VM...  40.2 us

profile of v5, /device:TPU:6, one launch (start us, length us, event | category | flops | bytes accessed | tf_op | source)
XLA Modules:
  0.0 41.5 jit_solution(1613506196099182660)
XLA Ops:
  0.6 40.2 %assimilate.1 = (f32[2,64,128]{2,1,0:T(8,128)S(1)}, f32[64,128]{1,0:T(8,128)S(1)}) custom-call(f32[2,64,128]{2,1,0:T(8,128)} %states.1, f32[64,128]{1,0:T(8,128)} %bed.1, f32[64,128]{1,0:T(8,128)} %background.1, s32[64,128]{1,0:T(8,128)} %mask.1, f32[64,128]{1,0:T(8,128)} %rate.1, s32[2,1,1,512]{3,2,1,0:T(1,128)} %cells.1, f32[2,1,1,512]{3,2,1,0:T(1,128)} %values.1), custom_call_target="tpu_custom_call" | custom-call | tf_op jit(solution)/shard_map/assimilate/pallas_call | solution.py:637
  40.8 0.7 %emit.1 = (f32[2,64,128]{2,1,0:T(8,128)}, f32[64,128]{1,0:T(8,128)}) custom-call(f32[2,64,128]{2,1,0:T(8,128)S(1)} %get-tuple-element.4.states, f32[64,128]{1,0:T(8,128)S(1)} %get-tuple-element.5.bed), custom_call_target="tpu_custom_call" | custom-call | tf_op jit(solution)/shard_map/emit/pallas_call | solution.py:667
